TPU v7x, 128 devices: a whole 4x4x4 slice. The times are simulated.
128 devices in a mesh: pipe: 8 (over z_lo, y), dp: 8 (over x, z_hi), tensor: 2 (over core).
Axes of the slice: x: 4, y: 4, z: 4 (z_hi: 2, z_lo: 2; z = z_hi * 2 + z_lo), core: 2. Of those that a mesh axis runs over, the one named last changes fastest.
Arguments:
- section_inputs: bfloat16 [8, 1024, 5120], P('pipe', 'dp'), may hold values from -6 to 6
- output_grad: bfloat16 [8, 1024, 5120], P('pipe', 'dp'), may hold values from -6 to 6
- norm_gain: float32 [8, 5120], P('pipe'), may hold values from 0.5 to 1.5
- weight: bfloat16 [8, 5120, 5120], P('pipe', 'tensor', 'dp'), may hold values from -0.078125 to 0.078125
- parked: bfloat16 [8, 3, 8, 16, 16, 5120], P('pipe', None, None, 'dp'), may hold values from -6 to 6
- in_flight: int32 [8], replicated, may hold values from 1 to 3
- old_hosts: int32 [8, 64, 1], P('pipe', 'dp'), may hold values from 0 to 7; in each aligned block of 8 rows (0 to 7, 8 to 15, ..., all dimensions but the last counted through in order) at most 2 rows name the same one
- new_hosts: int32 [8, 64, 1], P('pipe', 'dp'), may hold values from 0 to 7; in each aligned block of 8 rows (0 to 7, 8 to 15, ..., all dimensions but the last counted through in order) at most 2 rows name the same one
Outputs:
- section_output: bfloat16 [8, 1024, 5120], P('pipe', 'dp')
- input_grad: bfloat16 [8, 1024, 5120], P('pipe', 'dp')
- weight_grad: float32 [8, 5120, 5120], P('pipe', 'tensor', 'dp')
- gain_grad: float32 [8, 5120], P('pipe')
- parked_next: bfloat16 [8, 8, 16, 16, 5120], P('pipe', None, 'dp')
Inputs may be any that keep to these rules, and one draw needn't show every extreme that they name: `old_hosts`: within the 8 blocks of one device no host section is named more than 2 times, and some host section is named exactly 2 times. `new_hosts`: within the 8 blocks of one device no host section is named more than 2 times, and some host section is named exactly 2 times.
All inputs are finite; a program needn't handle non-finite values.
Results may differ from a plain program's by a relative error of at most 0.0052.
Values may be sent and summed in bfloat16 or wider, within the bound.
A program may use at most 192 MiB of HBM per device.

v0:
```python
import jax
import jax.numpy as jnp
from jax import lax
from jax.sharding import PartitionSpec as P

eps = 1e-05


def apply_norm(rows):
    values = rows.astype(jnp.float32)
    scale = lax.rsqrt(jnp.mean(values * values, axis=-1, keepdims=True) + eps)
    return (values * scale, scale)


def block_ranks(routes):
    count = routes.shape[-1]
    same = routes[..., :, None] == routes[..., None, :]
    order = jnp.arange(count, dtype=jnp.int32)
    before = order[None, :] < order[:, None]
    return jnp.sum(jnp.where(same & before, 1, 0), axis=-1).astype(jnp.int32)


def local(section_inputs, output_grad, norm_gain, weight, parked, in_flight, old_hosts, new_hosts):
    input_batch = section_inputs[0]
    grads = output_grad[0]
    scale_gain = norm_gain[0]
    w_local = weight[0]
    tok_rows, width = input_batch.shape
    halves = lax.axis_size("tensor")
    half_width = width // halves
    tensor_pos = lax.axis_index("tensor")
    sections = lax.axis_size("pipe")
    hosts_old = old_hosts[0, :, 0]
    hosts_new = new_hosts[0, :, 0]
    blocks = hosts_old.shape[0]
    rows_block = tok_rows // blocks
    stash = parked[0]
    slot_count = stash.shape[0]
    capacity = stash.shape[2]
    picked = jnp.arange(slot_count, dtype=jnp.int32)[:, None] == (in_flight - 1)[None, :]
    chosen = jnp.sum(
        jnp.where(picked[:, :, None, None, None], stash, jnp.zeros((), stash.dtype)), axis=0
    )
    returned = lax.all_to_all(chosen, "pipe", split_axis=0, concat_axis=0, tiled=True)
    flat_back = returned.reshape(sections * capacity, rows_block, width)
    old_index = hosts_old * capacity + block_ranks(hosts_old)
    earlier = flat_back[old_index].reshape(tok_rows, width)
    placed = jnp.zeros((sections * capacity, rows_block, width), jnp.bfloat16)
    new_index = hosts_new * capacity + block_ranks(hosts_new)
    placed = placed.at[new_index].set(input_batch.reshape(blocks, rows_block, width))
    parked_next = lax.all_to_all(
        placed.reshape(sections, capacity, rows_block, width),
        "pipe",
        split_axis=0,
        concat_axis=0,
        tiled=True,
    )
    centered_input, unused_value = apply_norm(input_batch)
    norm_output = (centered_input * scale_gain).astype(jnp.bfloat16)
    normed_half = lax.dynamic_slice_in_dim(norm_output, tensor_pos * half_width, half_width, 1)
    partial_cols = jnp.dot(
        lax.all_gather(normed_half, "dp", axis=0, tiled=True),
        w_local,
        preferred_element_type=jnp.float32,
    )
    summed = lax.psum(partial_cols, "tensor").astype(jnp.bfloat16)
    update = lax.all_to_all(summed, "dp", split_axis=0, concat_axis=1, tiled=True)
    section_output = (input_batch.astype(jnp.float32) + update.astype(jnp.float32)).astype(
        jnp.bfloat16
    )
    grad_cols = lax.all_to_all(grads, "dp", split_axis=1, concat_axis=0, tiled=True)
    old_hat, old_scale = apply_norm(earlier)
    old_normed = (old_hat * scale_gain).astype(jnp.bfloat16)
    old_half = lax.dynamic_slice_in_dim(old_normed, tensor_pos * half_width, half_width, 1)
    weight_grad = lax.dot_general(
        lax.all_gather(old_half, "dp", axis=0, tiled=True),
        grad_cols,
        (((0,), (0,)), ((), ())),
        preferred_element_type=jnp.float32,
    )
    half_grad = lax.psum_scatter(
        lax.dot_general(
            grad_cols, w_local, (((1,), (1,)), ((), ())), preferred_element_type=jnp.float32
        ),
        "dp",
        scatter_dimension=0,
        tiled=True,
    )
    normed_grad = lax.all_gather(half_grad, "tensor", axis=1, tiled=True)
    gain_term = jnp.sum(normed_grad * old_hat, axis=0)
    gain_grad = lax.psum(gain_term, "dp")
    scaled = normed_grad * scale_gain
    centred = scaled - old_hat * jnp.mean(scaled * old_hat, axis=1, keepdims=True)
    input_grad = (grads.astype(jnp.float32) + old_scale * centred).astype(jnp.bfloat16)
    return (
        section_output[None],
        input_grad[None],
        weight_grad[None],
        gain_grad[None],
        parked_next[None],
    )


def solution(mesh):
    in_specs = (
        P("pipe", "dp", None),
        P("pipe", "dp", None),
        P("pipe", None),
        P("pipe", "tensor", "dp"),
        P("pipe", None, None, "dp", None, None),
        P(),
        P("pipe", "dp", None),
        P("pipe", "dp", None),
    )
    out_specs = (
        P("pipe", "dp", None),
        P("pipe", "dp", None),
        P("pipe", "tensor", "dp"),
        P("pipe", None),
        P("pipe", None, "dp", None, None),
    )
    return jax.shard_map(local, mesh=mesh, in_specs=in_specs, out_specs=out_specs, check_vma=False)
```

profile of v0, /device:TPU:9, one launch (start us, length us, event | category | flops | bytes accessed | tf_op | source)
XLA Modules:
  0.0 450.7 jit_solution(7969775600485110885)
XLA Ops:
  7.2 2.6 copy.19
  9.8 25.5 %all_to_all.42 = bf16[128,8,640]{0,2,1:T(8,128)(2,1)} all-to-all(bf16[128,8,640]{0,2,1:T(8,128)(2,1)} %bitcast.66), channel_id=1, replica_groups=mesh['pipe'=8,'dp'=8,'tensor'=2] {'dp'}, dimensions={1} | all-to-all | bytes 2621440 | tf_op jit(solution)/shard_map/all_to_all | solution.py:71
  35.3 2.4 copy.20
  37.7 8.2 %fusion.1 = f32[1024,2560]{1,0:T(8,128)} fusion(bf16[1024,640]{1,0:T(8,128)(2,1)} %bitcast.68, bf16[1,2560,640]{2,1,0:T(8,128)(2,1)S(1)} %copy-done), kind=kOutput, calls=%fused_computation.5 | convolution fusion | flops 3355443200 | bytes 15073280 | tf_op jit(solution)/shard_map/dot_general | solution.py:82
  46.6 7.6 %fusion = bf16[8,2,16,5120]{3,2,1,0:T(8,128)(2,1)} fusion(bf16[1,3,8,2,16,5120]{5,4,3,2,1,0:T(8,128)(2,1)} %param.12, pred[3,8]{1,0:T(4,128)(4,1)S(1)} %iota_compare_fusion.1), kind=kLoop, calls=%fused_computation.3 | loop fusion | flops 6553600 | bytes 10485784 | tf_op jit(solution)/shard_map/reduce_sum | solution.py:41
  54.2 4.9 %all-to-all-start.1 = ((bf16[8,2,16,5120]{3,2,1,0:T(8,128)(2,1)}), bf16[8,2,16,5120]{3,2,1,0:T(8,128)(2,1)}, u32[]{:S(2)}, u32[]{:S(2)}) async-start(bf16[8,2,16,5120]{3,2,1,0:T(8,128)(2,1)} %fusion), calls=%async_computation.1 | async-start | bytes 5242880 | tf_op jit(solution)/shard_map/all_to_all | solution.py:44
  59.1 147.9 %reduce-scatter.2.cloned.1.call-done = f32[128,2560]{1,0:T(8,128)} async-done(((f32[1024,2560]{1,0:T(8,128)}), f32[128,2560]{1,0:T(8,128)}) %reduce-scatter.2.cloned.1.call-update) | async-done | bytes 1310736 | tf_op jit(solution)/shard_map/reduce_scatter | solution.py:81
  209.1 3.1 convert_bitcast_fusion
  212.2 3.4 gather_fusion
  217.5 4.2 all-gather.6.cloned.1.call-done
  221.7 3.3 multiply_reduce_fusion
  228.9 3.5 scatter_fusion
  232.4 41.9 %all_to_all.43 = bf16[8,2,16,5120]{3,2,1,0:T(8,128)(2,1)} all-to-all(bf16[8,2,16,5120]{3,2,1,0:T(8,128)(2,1)} %bitcast.63), channel_id=1, replica_groups=mesh['pipe'=8,'dp'=8,'tensor'=2] {'pipe'}, dimensions={0} | all-to-all | bytes 5242880 | tf_op jit(solution)/shard_map/all_to_all | solution.py:51
  274.3 60.4 %all-gather.4.cloned.1.call-done = bf16[1024,2560]{1,0:T(8,128)(2,1)} async-done(((bf16[128,2560]{1,0:T(8,128)(2,1)}), bf16[1024,2560]{1,0:T(8,128)(2,1)}) %all-gather.4.cloned.1.call-update) | async-done | bytes 5242896 | tf_op jit(solution)/shard_map/all_gather | solution.py:62
  334.7 8.2 %fusion.3 = f32[1024,640]{1,0:T(8,128)} fusion(bf16[1024,2560]{1,0:T(8,128)(2,1)} %all-gather.4.cloned.1.call-done, bf16[1,2560,640]{2,1,0:T(8,128)(2,1)S(1)} %copy-done), kind=kOutput, calls=%fused_computation.7 | convolution fusion | flops 3355443200 | bytes 11141120 | tf_op jit(solution)/shard_map/dot_general | solution.py:61
  342.9 12.5 %all-reduce.1 = bf16[1024,640]{1,0:T(8,128)(2,1)} all-reduce(f32[1024,640]{1,0:T(8,128)} %fusion.3), channel_id=1, replica_groups=mesh['pipe'=8,'dp'=8,'tensor'=2] {'tensor'}, use_global_device_ids=true, to_apply=%region_1.2 | all-reduce | flops 655360 | bytes 3932160 | tf_op jit(solution)/shard_map/psum | solution.py:66
  355.4 4.4 all-to-all-start
  359.8 3.6 fusion.7
  363.5 42.5 %psum.15 = f32[1,5120]{1,0:T(1,128)} all-reduce(f32[1,5120]{1,0:T(1,128)S(1)} %bitcast.73), channel_id=1, replica_groups=mesh['pipe'=8,'dp'=8,'tensor'=2] {'dp'}, use_global_device_ids=true, to_apply=%region_8.9 | all-reduce | flops 5120 | bytes 40960 | tf_op jit(solution)/shard_map/psum | solution.py:91
  405.9 15.2 %all-gather.8.cloned.1.call-done = bf16[1024,2560]{1,0:T(8,128)(2,1)} async-done(((bf16[128,2560]{1,0:T(8,128)(2,1)}), bf16[1024,2560]{1,0:T(8,128)(2,1)}) %all-gather.8.cloned.1.call-update) | async-done | bytes 5242896 | tf_op jit(solution)/shard_map/all_gather | solution.py:76
  421.1 10.0 %convolution_bitcast_fusion = f32[1,2560,640]{2,1,0:T(8,128)} fusion(bf16[1024,2560]{1,0:T(8,128)(2,1)} %all-gather.8.cloned.1.call-done, bf16[1024,640]{1,0:T(8,128)(2,1)} %bitcast.69), kind=kOutput, calls=%fused_computation.4 | convolution fusion | flops 3355443200 | bytes 13107200 | tf_op jit(solution)/shard_map/dot_general | solution.py:75
  432.6 3.0 copy.18
  435.6 3.5 reshape.152
  439.1 3.6 fusion.5
  (48 shorter events, 11.5 us)
Async XLA Ops:
  7.2 30.6 %copy-start = (bf16[1,2560,640]{2,1,0:T(8,128)(2,1)S(1)}, bf16[1,2560,640]{2,1,0:T(8,128)(2,1)}, u32[]{:S(2)}) copy-start(bf16[1,2560,640]{2,1,0:T(8,128)(2,1)} %param.11) | copy-start | bytes 9830404
  7.2 199.9 %reduce-scatter.2.cloned.1.call-start = ((), (), s32[]{:S(2)}) async-start(), calls=%async_computation.6 | async-start | bytes 11796480 | tf_op jit(solution)/shard_map/reduce_scatter | solution.py:81
  45.9 0.7 copy-start.7
  54.2 153.0 %copy-start.6 = (f32[1,5120]{1,0:T(1,128)S(1)}, f32[1,5120]{1,0:T(1,128)}, u32[]{:S(2)}) copy-start(f32[1,5120]{1,0:T(1,128)} %param.10) | copy-start | bytes 61444
  54.2 153.0 %copy-start.8 = (s32[1,8,1]{1,2,0:T(1,128)S(1)}, s32[1,8,1]{1,2,0:T(1,128)}, u32[]{:S(2)}) copy-start(s32[1,8,1]{1,2,0:T(1,128)} %param.14) | copy-start | bytes 100
  54.2 158.0 %all-to-all-start.1 = ((bf16[8,2,16,5120]{3,2,1,0:T(8,128)(2,1)}), bf16[8,2,16,5120]{3,2,1,0:T(8,128)(2,1)}, u32[]{:S(2)}, u32[]{:S(2)}) async-start(bf16[8,2,16,5120]{3,2,1,0:T(8,128)(2,1)} %fusion), calls=%async_computation.1 | async-start | bytes 5242880 | tf_op jit(solution)/shard_map/all_to_all | solution.py:44
  59.1 162.5 %all-gather.6.cloned.1.call-start = ((), (), s32[]{:S(2)}) async-start(), calls=%async_computation.7 | async-start | bytes 3932160 | tf_op jit(solution)/shard_map/all_gather | solution.py:89
  207.1 127.7 %all-gather.4.cloned.1.call-start = ((), (), s32[]{:S(2)}) async-start(), calls=%async_computation.5 | async-start | bytes 5898240 | tf_op jit(solution)/shard_map/all_gather | solution.py:62
  221.7 3.3 copy-start.4
  225.0 1.9 copy-start.9
  226.3 194.8 %all-gather.8.cloned.1.call-start = ((), (), s32[]{:S(2)}) async-start(), calls=%async_computation.8 | async-start | bytes 5898240 | tf_op jit(solution)/shard_map/all_gather | solution.py:76
  342.9 16.9 %copy-start.2 = (bf16[8,16,5120]{2,1,0:T(8,128)(2,1)S(1)}, bf16[8,16,5120]{2,1,0:T(8,128)(2,1)}, u32[]{:S(2)}) copy-start(bf16[8,16,5120]{2,1,0:T(8,128)(2,1)} %gather_fusion) | copy-start | bytes 3932164
  342.9 16.9 %copy-start.5 = (bf16[1,128,5120]{2,1,0:T(8,128)(2,1)S(1)}, bf16[1,128,5120]{2,1,0:T(8,128)(2,1)}, u32[]{:S(2)}) copy-start(bf16[1,128,5120]{2,1,0:T(8,128)(2,1)} %param.9) | copy-start | bytes 3932164
  355.4 75.7 %all-to-all-start = ((bf16[8,128,640]{2,1,0:T(8,128)(2,1)}), bf16[8,128,640]{2,1,0:T(8,128)(2,1)}, u32[]{:S(2)}, u32[]{:S(2)}) async-start(bf16[8,128,640]{2,1,0:T(8,128)(2,1)} %bitcast.67), calls=%async_computation | async-start | bytes 2621440 | tf_op jit(solution)/shard_map/all_to_all | solution.py:67
  439.1 3.6 copy-start.3
  439.1 5.1 %copy-start.1 = (bf16[1,2560,640]{2,1,0:T(8,128)(2,1)S(1)}, bf16[1,2560,640]{2,1,0:T(8,128)(2,1)}, u32[]{:S(2)}) copy-start(bf16[1,2560,640]{2,1,0:T(8,128)(2,1)} %param.11) | copy-start | bytes 9830404
Sparse Core Ops, SparseCore 0:
  46.0 160.9 reduce-scatter.1
  208.8 12.8 all-gather.5
  226.4 108.2 all-gather.3
  337.7 83.3 all-gather.7
where the time goes:
time: 453 us; the launch traced here: 451 us
  waiting for transfers between devices  228 us (50%)
  blocking collectives  122 us (27%)
  other arithmetic  27.8 us (6%)
  matrix products  26.3 us (6%)
  local copies, waits for them, and re-layouts  22.6 us (5%)
  between operations  13.9 us (3%)
  starting transfers between devices  9.5 us (2%)
    reduce_scatter x1, waiting for transfers between devices, local(): lax.psum_scatter(lax.dot_general(grad_cols, w_local, (((1,), (1,)), ((),...  148 us
    all_gather x1, waiting for transfers between devices, local(): lax.all_gather(normed_half, 'dp', axis=0, tiled=True)  60.4 us
    psum x1, blocking collectives, local(): gain_grad = lax.psum(gain_term, 'dp')  42.5 us
    all_to_all x1, blocking collectives, local(): lax.all_to_all(placed.reshape(sections, capacity, rows_block, width), 'pi...  41.9 us
    all_to_all x1, blocking collectives, local(): lax.all_to_all(grads, 'dp', split_axis=1, concat_axis=0, tiled=True)  25.5 us
    all_gather x1, waiting for transfers between devices, local(): lax.all_gather(old_half, 'dp', axis=0, tiled=True)  15.2 us
    psum x1, blocking collectives, local(): summed = lax.psum(partial_cols, 'tensor').astype(jnp.bfloat16)  12.5 us
    dot_general x1, matrix products, local(): lax.dot_general(lax.all_gather(old_half, 'dp', axis=0, tiled=True), grad_...  9.96 us
  transfers between devices with their start and end apart: 6, of which 4 were waited for; matrix products, arithmetic and copies ran while one was open for 10% of the time, Pallas kernels for 0%

commit v1 on v0

v1 whole, which is shorter than its diff:
```python
import functools

import jax
import jax.numpy as jnp
from jax import lax
from jax.experimental import pallas as pl
from jax.experimental.pallas import tpu as pltpu
from jax.sharding import PartitionSpec as P

eps = 1e-05
MESH = pl.DeviceIdType.MESH
X = 4
CT = 512


def kernel(
    x_hbm, blocks_hbm, grad_hbm, gain_hbm, w_hbm, parked_hbm, flight, hosts_old, hosts_new,
    so_hbm, ig_hbm, wg_hbm, gg_hbm, pn_hbm,
    xf, xh, gh, gain, w, stage, p1s, p1r, early, oscale, p2s, gc,
    agx, ago, a2, b_r, b_l, rl2, rr2, rl1, rr1, zs, zr, ng,
    part, sib_part, up, ur, us, uin, so, ig, wg, gp, gsum,
    local_sem, a2a_s, a2a_r, p1_s, p1_r, p2_s, p2_r, agx_s, agx_r, ago_s, ago_r,
    rs_s, rs_r, sib_s, sib_r, up_s, up_r, gg_s, gg_r, out_sem,
):
    f32, bf16 = jnp.float32, jnp.bfloat16
    p = lax.axis_index("pipe")
    d = lax.axis_index("dp")
    c = lax.axis_index("tensor")
    xi, zh = d // 2, lax.rem(d, 2)
    o = 1 - c
    xr, xl, x2 = lax.rem(xi + 1, X), lax.rem(xi + 3, X), lax.rem(xi + 2, X)
    dz = xi * 2 + (1 - zh)
    dr, dl = xr * 2 + zh, xl * 2 + zh
    drz, dlz = xr * 2 + (1 - zh), xl * 2 + (1 - zh)
    hc = xh.shape[-1]
    oc = gc.shape[-1]
    right, left, zdev = (p, dr, c), (p, dl, c), (p, dz, c)
    sib = (p, d, o)
    half_c = pl.ds(pl.multiple_of(c * hc, 128), hc)

    def pipe_peer(k):
        return lax.rem(p + k, 8)

    def dp_peer(k):
        return lax.rem(d + k, 8)

    sends = []

    def remote(src, dst, ssem, rsem, dev):
        cp = pltpu.make_async_remote_copy(
            src_ref=src, dst_ref=dst, send_sem=ssem, recv_sem=rsem,
            device_id=dev, device_id_type=MESH,
        )
        cp.start()
        sends.append(cp)
        return cp

    def landed(dst, rsem):
        pltpu.make_async_copy(dst, dst, rsem).wait()

    def local(src, dst, sem):
        cp = pltpu.make_async_copy(src, dst, sem)
        cp.start()
        return cp

    c_xf = local(x_hbm, xf, local_sem.at[0])
    c_xh = local(blocks_hbm.at[:, :, half_c], xh.at[pl.ds(0, 8)], local_sem.at[1])
    c_gain = local(gain_hbm.at[:, half_c], gain, local_sem.at[2])
    c_stage = local(parked_hbm.at[:, :, :, :, half_c], stage, local_sem.at[3])
    c_w = local(w_hbm, w, local_sem.at[4])
    c_gh = local(grad_hbm.at[:, half_c], gh, local_sem.at[5])

    barrier = pltpu.get_barrier_semaphore()
    for k in range(1, 8):
        pl.semaphore_signal(barrier, inc=1, device_id=(pipe_peer(k), d, c), device_id_type=MESH)
        pl.semaphore_signal(barrier, inc=1, device_id=(p, dp_peer(k), c), device_id_type=MESH)
    pl.semaphore_signal(barrier, inc=1, device_id=sib, device_id_type=MESH)
    pl.semaphore_wait(barrier, 15)

    for k in (2, 6, 1, 3, 5, 7, 4):
        q = dp_peer(k)
        remote(
            grad_hbm.at[pl.ds(c * 64, 64), pl.ds(pl.multiple_of(q * oc, 128), oc)],
            gc.at[d, c], a2a_s.at[k], a2a_r.at[k], (p, q, c),
        )
    c_gown = local(
        grad_hbm.at[pl.ds(c * 64, 64), pl.ds(pl.multiple_of(d * oc, 128), oc)],
        gc.at[d, c], local_sem.at[6],
    )

    def gather_start(buf, ss, rs):
        remote(buf.at[d], buf.at[d], ss.at[0], rs.at[0], zdev)
        remote(buf.at[d], buf.at[d], ss.at[1], rs.at[1], right)
        remote(buf.at[d], buf.at[d], ss.at[3], rs.at[3], left)

    def gather_z(buf, ss, rs):
        landed(buf.at[dz], rs.at[0])
        remote(buf.at[dz], buf.at[dz], ss.at[2], rs.at[2], right)
        remote(buf.at[dz], buf.at[dz], ss.at[4], rs.at[4], left)

    def gather_forward(buf, ss, rs, at, from_left, from_right):
        landed(buf.at[from_left], rs.at[1 + at])
        remote(buf.at[from_left, 0], buf.at[from_left, 0], ss.at[5 + at], rs.at[5 + at], right)
        landed(buf.at[from_right], rs.at[3 + at])
        remote(buf.at[from_right, 1], buf.at[from_right, 1], ss.at[7 + at], rs.at[7 + at], left)

    def gather_end(buf, rs):
        for at in range(2):
            landed(buf.at[0, 0], rs.at[5 + at])
            landed(buf.at[0, 1], rs.at[7 + at])

    c_xf.wait()
    c_xh.wait()
    c_gain.wait()

    def norm_rows(i, _):
        rows = pl.ds(pl.multiple_of(i * 16, 16), 16)
        v = xf[rows, :].astype(f32)
        scale = lax.rsqrt(jnp.mean(v * v, axis=-1, keepdims=True) + eps)
        val = (xh[i].astype(f32) * scale * gain[...]).astype(bf16)
        agx[d, i // 4, pl.ds(pl.multiple_of(lax.rem(i, 4) * 16, 16), 16), :] = val
        return 0

    lax.fori_loop(0, 8, norm_rows, 0)
    gather_start(agx, agx_s, agx_r)

    c_stage.wait()

    def pick(s, _):
        p1s[s] = stage[jnp.maximum(flight[s] - 1, 0), s]
        return 0

    lax.fori_loop(0, 8, pick, 0)
    for k in range(1, 8):
        q = pipe_peer(k)
        remote(p1s.at[q], p1r.at[pl.ds(p * 2, 2)], p1_s.at[k], p1_r.at[k], (q, d, c))
    c_p1own = local(p1s.at[p], p1r.at[pl.ds(p * 2, 2)], local_sem.at[7])

    def place(hosts):
        h = [hosts[b] for b in range(8)]
        return [
            h[b] * 2 + sum([jnp.where(h[a] == h[b], 1, 0) for a in range(b)], jnp.int32(0))
            for b in range(8)
        ]

    xh[8] = jnp.zeros((16, hc), bf16)
    new_at = place(hosts_new)
    old_at = place(hosts_old)

    for slot in range(16):
        which = 8 + sum([jnp.where(new_at[b] == slot, b - 8, 0) for b in range(8)], jnp.int32(0))
        p2s[slot // 2, slot % 2] = xh[which]
    for k in range(1, 8):
        q = pipe_peer(k)
        remote(p2s.at[q], pn_hbm.at[p, :, :, half_c], p2_s.at[k], p2_r.at[k], (q, d, c))
    c_p2own = local(p2s.at[p], pn_hbm.at[p, :, :, half_c], local_sem.at[8])

    c_gown.wait()
    for k in range(1, 8):
        landed(gc.at[lax.rem(d + 8 - k, 8), c], a2a_r.at[k])
    remote(gc.at[:, c], gc.at[:, c], sib_s.at[0], sib_r.at[0], sib)
    c_w.wait()
    landed(gc.at[:, o], sib_r.at[0])

    def back(rows, t):
        return lax.dot_general(
            rows, w[pl.ds(pl.multiple_of(t * CT, CT), CT), :],
            (((1,), (1,)), ((), ())), preferred_element_type=f32,
        )

    def cols(t):
        return pl.ds(pl.multiple_of(t * CT, CT), CT)

    n_t = hc // CT

    def far(t, _):
        val = back(gc[pl.ds(x2 * 2, 2)].reshape(256, oc), t)
        a2[:, :, :, cols(t)] = val.astype(bf16).reshape(2, 2, 64, CT)
        return 0

    lax.fori_loop(0, n_t, far, 0)
    for j in range(2):
        remote(a2.at[j, 0], rl2.at[j], rs_s.at[j], rs_r.at[j], right)
        remote(a2.at[j, 1], rr2.at[j], rs_s.at[2 + j], rs_r.at[2 + j], left)

    def near(t, _):
        val = back(gc[pl.ds(xr * 2, 2), 1].reshape(128, oc), t)
        b_r[:, 1, :, cols(t)] = val.astype(bf16).reshape(2, 64, CT)
        val = back(gc[pl.ds(xl * 2, 2), 0].reshape(128, oc), t)
        b_l[:, 0, :, cols(t)] = val.astype(bf16).reshape(2, 64, CT)
        return 0

    lax.fori_loop(0, n_t, near, 0)
    for j in range(2):
        remote(b_r.at[j, 1], rl1.at[j, 1], rs_s.at[4 + j], rs_r.at[4 + j], right)
        remote(b_l.at[j, 0], rr1.at[j, 0], rs_s.at[6 + j], rs_r.at[6 + j], left)

    gather_z(agx, agx_s, agx_r)

    c_p1own.wait()
    for k in range(1, 8):
        landed(p1r.at[pl.ds(lax.rem(p + 8 - k, 8) * 2, 2)], p1_r.at[k])
    for b in range(8):
        early[pl.ds(b * 16, 16), :] = p1r[old_at[b]]

    def lanes(v):
        total = v[:, 0:128]
        for i in range(1, v.shape[1] // 128):
            total = total + v[:, i * 128:(i + 1) * 128]
        return total

    def squares(i, _):
        rows = pl.ds(pl.multiple_of(i * 16, 16), 16)
        v = early[rows, :].astype(f32)
        part[0, rows, :] = lanes(v * v)
        return 0

    lax.fori_loop(0, 8, squares, 0)
    remote(part.at[0], sib_part.at[0], sib_s.at[1], sib_r.at[1], sib)
    landed(sib_part.at[0], sib_r.at[1])

    def norm_old(i, _):
        rows = pl.ds(pl.multiple_of(i * 16, 16), 16)
        sq = jnp.sum(part[0, rows, :] + sib_part[0, rows, :], axis=-1, keepdims=True)
        scale = lax.rsqrt(sq / (2 * hc) + eps)
        oscale[rows, :] = jnp.broadcast_to(scale, (16, 128))
        val = (early[rows, :].astype(f32) * scale * gain[...]).astype(bf16)
        ago[d, i // 4, pl.ds(pl.multiple_of(lax.rem(i, 4) * 16, 16), 16), :] = val
        return 0

    lax.fori_loop(0, 8, norm_old, 0)
    gather_start(ago, ago_s, ago_r)

    gather_forward(agx, agx_s, agx_r, 0, dl, dr)

    for j in range(2):
        landed(rl2.at[j], rs_r.at[j])
        landed(rr2.at[j], rs_r.at[2 + j])

    def through(t, _):
        val = back(gc[pl.ds(xr * 2, 2), 0].reshape(128, oc), t)
        val = val + rl2[:, :, cols(t)].reshape(128, CT).astype(f32)
        b_r[:, 0, :, cols(t)] = val.astype(bf16).reshape(2, 64, CT)
        val = back(gc[pl.ds(xl * 2, 2), 1].reshape(128, oc), t)
        val = val + rr2[:, :, cols(t)].reshape(128, CT).astype(f32)
        b_l[:, 1, :, cols(t)] = val.astype(bf16).reshape(2, 64, CT)
        return 0

    lax.fori_loop(0, n_t, through, 0)
    for j in range(2):
        remote(b_r.at[j, 0], rl1.at[j, 0], rs_s.at[8 + j], rs_r.at[8 + j], right)
        remote(b_l.at[j, 1], rr1.at[j, 1], rs_s.at[10 + j], rs_r.at[10 + j], left)

    gather_forward(agx, agx_s, agx_r, 1, dlz, drz)
    gather_z(ago, ago_s, ago_r)

    c_p2own.wait()
    for k in range(1, 8):
        landed(pn_hbm.at[lax.rem(p + 8 - k, 8), :, :, half_c], p2_r.at[k])
    remote(pn_hbm.at[:, :, :, half_c], pn_hbm.at[:, :, :, half_c], sib_s.at[2], sib_r.at[2], sib)

    def project(xq, i):
        two = pl.ds(xq * 2, 2)

        def body(t, _):
            val = jnp.dot(
                agx[two, :, :, cols(t)].reshape(256, CT), w[cols(t), :],
                preferred_element_type=f32,
            ).reshape(2, 2, 64, oc)

            @pl.when(t == 0)
            def _():
                up[two] = val

            @pl.when(t > 0)
            def _():
                up[two] = up[two] + val

            return 0

        lax.fori_loop(0, n_t, body, 0)
        remote(up.at[two, o], ur.at[two], up_s.at[i], up_r.at[i], sib)

    def project_sum(xq, i):
        two = pl.ds(xq * 2, 2)
        landed(ur.at[two], up_r.at[i])
        us[two] = (up[two, c] + ur[two]).astype(bf16)

    project(xi, 0)
    project(xl, 1)
    project(xr, 2)
    gather_forward(ago, ago_s, ago_r, 0, dl, dr)
    project_sum(xi, 0)
    project_sum(xl, 1)
    project_sum(xr, 2)
    remote(us.at[dz], uin.at[d], up_s.at[4], up_r.at[4], zdev)
    remote(us.at[dl], uin.at[d], up_s.at[5], up_r.at[5], left)
    remote(us.at[dr], uin.at[d], up_s.at[6], up_r.at[6], right)
    remote(us.at[dlz], uin.at[d], up_s.at[7], up_r.at[7], (p, dlz, c))
    remote(us.at[drz], uin.at[d], up_s.at[8], up_r.at[8], (p, drz, c))

    for j in range(2):
        landed(rl1.at[j, 1], rs_r.at[4 + j])
        landed(rr1.at[j, 0], rs_r.at[6 + j])
        landed(rl1.at[j, 0], rs_r.at[8 + j])
        landed(rr1.at[j, 1], rs_r.at[10 + j])

    def to_z(t, _):
        val = back(gc[dz].reshape(128, oc), t)
        val = val + rl1[1 - zh, :, :, cols(t)].reshape(128, CT).astype(f32)
        val = val + rr1[1 - zh, :, :, cols(t)].reshape(128, CT).astype(f32)
        zs[:, cols(t)] = val.astype(bf16)
        return 0

    lax.fori_loop(0, n_t, to_z, 0)
    remote(zs, zr, rs_s.at[12], rs_r.at[12], zdev)

    gather_end(agx, agx_r)
    project(x2, 3)
    gather_forward(ago, ago_s, ago_r, 1, dlz, drz)
    project_sum(x2, 3)
    for z in range(2):
        remote(us.at[x2 * 2 + z], uin.at[d], up_s.at[9 + z], up_r.at[9 + lax.rem(z + zh, 2)], (p, x2 * 2 + z, c))

    def weight_part(xq, first):
        two = pl.ds(xq * 2, 2)

        def body(t, _):
            val = lax.dot_general(
                ago[two, :, :, cols(t)].reshape(256, CT), gc[two].reshape(256, oc),
                (((0,), (0,)), ((), ())), preferred_element_type=f32,
            )
            if first:
                wg[cols(t), :] = val
            else:
                wg[cols(t), :] = wg[cols(t), :] + val
            return 0

        lax.fori_loop(0, n_t, body, 0)

    weight_part(xi, True)
    weight_part(xl, False)
    weight_part(xr, False)

    landed(zr, rs_r.at[12])
    part[1] = jnp.zeros((128, 128), f32)

    def own(t, _):
        val = back(gc[d].reshape(128, oc), t)
        val = val + rl1[zh, :, :, cols(t)].reshape(128, CT).astype(f32)
        val = val + rr1[zh, :, :, cols(t)].reshape(128, CT).astype(f32)
        val = val + zr[:, cols(t)].astype(f32)
        ng[:, cols(t)] = val
        term = val * (early[:, cols(t)].astype(f32) * oscale[:, 0:1])
        gp[d, :, cols(t)] = jnp.sum(term, axis=0, keepdims=True)
        part[1] = part[1] + lanes(term * gain[:, cols(t)])
        return 0

    lax.fori_loop(0, n_t, own, 0)
    remote(part.at[1], sib_part.at[1], sib_s.at[3], sib_r.at[3], sib)
    for k in range(1, 8):
        q = dp_peer(k)
        remote(gp.at[d], gp.at[d], gg_s.at[k], gg_r.at[k], (p, q, c))

    uin[d] = us[d]
    landed(uin.at[0], up_r.at[4])
    landed(uin.at[0], up_r.at[5])
    landed(uin.at[0], up_r.at[6])
    landed(uin.at[0], up_r.at[7])
    landed(uin.at[0], up_r.at[8])
    landed(uin.at[0], up_r.at[9])
    landed(uin.at[0], up_r.at[10])
    mine = pl.ds(pl.multiple_of(c * 64, 64), 64)

    def add_update(q, _):
        at = pl.ds(pl.multiple_of(q * oc, 128), oc)
        so[:, at] = (xf[mine, at].astype(f32) + uin[q].astype(f32)).astype(bf16)
        return 0

    lax.fori_loop(0, 8, add_update, 0)
    c_so = local(so, so_hbm.at[mine, :], out_sem.at[0])
    remote(so, so_hbm.at[mine, :], sib_s.at[4], sib_r.at[4], sib)

    landed(sib_part.at[1], sib_r.at[3])
    c_gh.wait()

    def input_rows(i, _):
        rows = pl.ds(pl.multiple_of(i * 16, 16), 16)
        mean = jnp.sum(part[1, rows, :] + sib_part[1, rows, :], axis=-1, keepdims=True) / (2 * hc)
        scale = oscale[rows, 0:1]
        old_hat = early[rows, :].astype(f32) * scale
        centred = ng[rows, :] * gain[...] - old_hat * mean
        ig[rows, :] = (gh[rows, :].astype(f32) + scale * centred).astype(bf16)
        return 0

    lax.fori_loop(0, 8, input_rows, 0)
    c_ig = local(ig, ig_hbm.at[:, half_c], out_sem.at[1])
    remote(ig, ig_hbm.at[:, half_c], sib_s.at[5], sib_r.at[5], sib)

    for k in range(1, 8):
        landed(gp.at[0], gg_r.at[k])
    total = gp[0]
    for q in range(1, 8):
        total = total + gp[q]
    gsum[...] = total
    c_gg = local(gsum, gg_hbm.at[:, half_c], out_sem.at[2])
    remote(gsum, gg_hbm.at[:, half_c], sib_s.at[6], sib_r.at[6], sib)

    gather_end(ago, ago_r)
    c_wg = []
    two2 = pl.ds(x2 * 2, 2)
    for t in range(n_t):
        at = pl.ds(t * CT, CT)
        val = lax.dot_general(
            ago[two2, :, :, at].reshape(256, CT), gc[two2].reshape(256, oc),
            (((0,), (0,)), ((), ())), preferred_element_type=f32,
        )
        wg[at, :] = wg[at, :] + val
        c_wg.append(local(wg.at[at, :], wg_hbm.at[at, :], out_sem.at[3 + t]))

    half_o = pl.ds(pl.multiple_of(o * hc, 128), hc)
    landed(pn_hbm.at[:, :, :, half_o], sib_r.at[2])
    landed(so_hbm.at[pl.ds(pl.multiple_of(o * 64, 64), 64), :], sib_r.at[4])
    landed(ig_hbm.at[:, half_o], sib_r.at[5])
    landed(gg_hbm.at[:, half_o], sib_r.at[6])
    for cp in [c_so, c_ig, c_gg] + c_wg:
        cp.wait()
    for cp in sends:
        cp.wait_send()


def local(section_inputs, output_grad, norm_gain, weight, parked, in_flight, old_hosts, new_hosts):
    rows, width = section_inputs.shape[1:]
    hc, oc = weight.shape[1:]
    f32, bf16 = jnp.float32, jnp.bfloat16
    hbm = pl.BlockSpec(memory_space=pl.ANY)
    smem = pl.BlockSpec(memory_space=pltpu.SMEM)
    vm = pltpu.VMEM
    dma = pltpu.SemaphoreType.DMA
    outs = pl.pallas_call(
        kernel,
        out_shape=(
            jax.ShapeDtypeStruct((rows, width), bf16),
            jax.ShapeDtypeStruct((rows, width), bf16),
            jax.ShapeDtypeStruct((hc, oc), f32),
            jax.ShapeDtypeStruct((1, width), f32),
            jax.ShapeDtypeStruct((8, 2, 16, width), bf16),
        ),
        in_specs=[hbm] * 6 + [smem] * 3,
        out_specs=(hbm,) * 5,
        scratch_shapes=[
            vm((rows, width), bf16),
            vm((9, 16, hc), bf16),
            vm((rows, hc), bf16),
            vm((1, hc), f32),
            vm((hc, oc), bf16),
            vm((3, 8, 2, 16, hc), bf16),
            vm((8, 2, 16, hc), bf16),
            vm((16, 16, hc), bf16),
            vm((rows, hc), bf16),
            vm((rows, 128), f32),
            vm((8, 2, 16, hc), bf16),
            vm((8, 2, 64, oc), bf16),
            vm((8, 2, 64, hc), bf16),
            vm((8, 2, 64, hc), bf16),
            vm((2, 2, 64, hc), bf16),
            vm((2, 2, 64, hc), bf16),
            vm((2, 2, 64, hc), bf16),
            vm((2, 64, hc), bf16),
            vm((2, 64, hc), bf16),
            vm((2, 2, 64, hc), bf16),
            vm((2, 2, 64, hc), bf16),
            vm((rows, hc), bf16),
            vm((rows, hc), bf16),
            vm((rows, hc), f32),
            vm((2, rows, 128), f32),
            vm((2, rows, 128), f32),
            vm((8, 2, 64, oc), f32),
            vm((8, 64, oc), f32),
            vm((8, 64, oc), bf16),
            vm((8, 64, oc), bf16),
            vm((64, width), bf16),
            vm((rows, hc), bf16),
            vm((hc, oc), f32),
            vm((8, 1, hc), f32),
            vm((1, hc), f32),
            dma((9,)),
            dma((8,)), dma((8,)),
            dma((8,)), dma((8,)),
            dma((8,)), dma((8,)),
            dma((9,)), dma((9,)),
            dma((9,)), dma((9,)),
            dma((13,)), dma((13,)),
            dma((7,)), dma((7,)),
            dma((11,)), dma((11,)),
            dma((8,)), dma((8,)),
            dma((8,)),
        ],
        compiler_params=pltpu.CompilerParams(
            collective_id=0, has_side_effects=True, vmem_limit_bytes=62 * 2**20
        ),
        cost_estimate=pl.CostEstimate(flops=10 * 2**30, bytes_accessed=40 * 2**20, transcendentals=0),
        name="relay_step",
    )(
        section_inputs[0], section_inputs[0].reshape(8, 16, width), output_grad[0], norm_gain, weight[0], parked[0],
        in_flight, old_hosts[0, :, 0], new_hosts[0, :, 0],
    )
    so, ig, wg, gg, pn = outs
    return so[None], ig[None], wg[None], gg, pn[None]


def solution(mesh):
    in_specs = (
        P("pipe", "dp", None),
        P("pipe", "dp", None),
        P("pipe", None),
        P("pipe", "tensor", "dp"),
        P("pipe", None, None, "dp", None, None),
        P(),
        P("pipe", "dp", None),
        P("pipe", "dp", None),
    )
    out_specs = (
        P("pipe", "dp", None),
        P("pipe", "dp", None),
        P("pipe", "tensor", "dp"),
        P("pipe", None),
        P("pipe", None, "dp", None, None),
    )
    return jax.shard_map(local, mesh=mesh, in_specs=in_specs, out_specs=out_specs, check_vma=False)
```

time: 453 us -> 178 us (0.39)
  waiting for transfers between devices: 228 us -> 0 us
  Pallas kernels: 0 us -> 165 us
  blocking collectives: 122 us -> 0 us
  other arithmetic: 27.8 us -> 0 us
  matrix products: 26.3 us -> 0 us
  between operations: 13.9 us -> 0.66 us
  local copies, waits for them, and re-layouts: 22.6 us -> 11.9 us
  starting transfers between devices: 9.5 us -> 0 us
    pallas_call x0 -> x1, Pallas kernels: none -> 165 us  [local(): pl.pallas_call(kernel, out_shape=(jax.ShapeDtypeStruct((rows, width), bf1...]
    reduce_scatter x1 -> x0, waiting for transfers between devices: 148 us -> none  [local(): lax.psum_scatter(lax.dot_general(grad_cols, w_local, (((1,), (1,)), ((),...]
    all_gather x3 -> x0, waiting for transfers between devices: 79.8 us -> none  [the longest x1 60.4 us: local(): lax.all_gather(normed_half, 'dp', axis=0, tiled=True)]
    all_to_all x2 -> x0, blocking collectives: 67.4 us -> none  [the longest x1 41.9 us: local(): lax.all_to_all(placed.reshape(sections, capacity, rows_block, width), 'pi...]
    psum x2 -> x0, blocking collectives: 54.9 us -> none  [the longest x1 42.5 us: local(): gain_grad = lax.psum(gain_term, 'dp')]
    dot_general x3 -> x0, matrix products: 26.3 us -> none  [the longest x1 9.96 us: local(): lax.dot_general(lax.all_gather(old_half, 'dp', axis=0, tiled=True), grad_...]
    reduce_sum x6 -> x0, other arithmetic: 14.7 us -> none  [the longest x1 7.59 us: local(): jnp.sum(jnp.where(picked[:, :, None, None, None], stash, jnp.zeros((), st...]
    convert_element_type x4 -> x0, other arithmetic: 9.44 us -> none  [the longest x1 3.57 us: local(): (input_batch.astype(jnp.float32) + update.astype(jnp.float32)).astype(jnp...]
  transfers between devices with their start and end apart: 6 -> 0, of which waited for: 4 -> 0; matrix products, arithmetic and copies ran while one was open for 10% -> 0% of each run, Pallas kernels for 0% -> 0%
where the time goes in v1:
time: 178 us
  Pallas kernels  165 us (93%)
  local copies, waits for them, and re-layouts  11.9 us (7%)
    pallas_call x1, Pallas kernels, local(): pl.pallas_call(kernel, out_shape=(jax.ShapeDtypeStruct((rows, width), bf1...  165 us
    unnamed x11, local copies, waits for them, and re-layouts  11.9 us

profile of v1, /device:TPU:9, one launch (start us, length us, event | category | flops | bytes accessed | tf_op | source)
XLA Modules:
  0.0 177.9 jit_solution(3460816158511160736)
XLA Ops:
  0.6 165.3 %relay_step.1 = (bf16[128,5120]{1,0:T(8,128)(2,1)}, bf16[128,5120]{1,0:T(8,128)(2,1)}, f32[2560,640]{1,0:T(8,128)}, f32[1,5120]{1,0:T(1,128)}, bf16[8,2,16,5120]{3,2,1,0:T(8,128)(2,1)}) custom-call(bf16[128,5120]{1,0:T(8,128)(2,1)} %bitcast.17, bf16[8,16,5120]{2,1,0:T(8,128)(2,1)} %bitcast.18, bf16[128,5120]{1,0:T(8,128)(2,1)} %bitcast.19, ...), custom_call_target="tpu_custom_call" | custom-call | flops 10737418240 | bytes 41943040 | tf_op jit(solution)/shard_map/relay_step/pallas_call | solution.py:440
  165.9 0.0 copy-start.1
  165.9 2.6 %copy.18 = bf16[1,128,5120]{2,1,0:T(8,128)(2,1)} copy(bf16[1,128,5120]{2,1,0:T(8,128)(2,1)} %bitcast.14) | data formatting | bytes 2621440
  168.5 0.0 copy-done.1
  168.5 1.1 copy.19
  169.6 0.0 copy-start.2
  169.6 0.0 copy-start
  169.6 6.2 %copy.20 = f32[1,2560,640]{2,1,0:T(8,128)} copy(f32[1,2560,640]{2,1,0:T(8,128)} %bitcast.11) | data formatting | bytes 13107200
  175.8 0.0 copy-done.2
  175.8 0.6 copy.21
  176.4 0.0 copy-done
  176.4 1.5 copy.22
Async XLA Ops:
  165.9 2.6 %copy-start.1 = (bf16[128,5120]{1,0:T(8,128)(2,1)S(1)}, bf16[128,5120]{1,0:T(8,128)(2,1)}, u32[]{:S(2)}) copy-start(bf16[128,5120]{1,0:T(8,128)(2,1)} %get-tuple-element.11) | copy-start | bytes 3932164
  169.6 6.2 %copy-start.2 = (f32[1,5120]{1,0:T(1,128)S(1)}, f32[1,5120]{1,0:T(1,128)}, u32[]{:S(2)}) copy-start(f32[1,5120]{1,0:T(1,128)} %get-tuple-element.23) | copy-start | bytes 61444
  169.6 6.8 %copy-start = (bf16[8,2,16,5120]{3,2,1,0:T(8,128)(2,1)S(1)}, bf16[8,2,16,5120]{3,2,1,0:T(8,128)(2,1)}, u32[]{:S(2)}) copy-start(bf16[8,2,16,5120]{3,2,1,0:T(8,128)(2,1)} %get-tuple-element.14) | copy-start | bytes 7864324

commit v2 on v0

v2 whole, which is shorter than its diff:
```python
import functools

import jax
import jax.numpy as jnp
from jax import lax
from jax.experimental import pallas as pl
from jax.experimental.pallas import tpu as pltpu
from jax.sharding import PartitionSpec as P

eps = 1e-05
MESH = pl.DeviceIdType.MESH
X = 4
CT = 512


def kernel(
    x_hbm, blocks_hbm, grad_hbm, gain_hbm, w_hbm, parked_hbm, flight, hosts_old, hosts_new,
    so_hbm, ig_hbm, wg_hbm, gg_hbm, pn_hbm, ago2_hbm, gc2_hbm,
    xf, xh, gh, gain, w, stage, p1s, p1r, early, oscale, p2s, p2r, gc,
    agx, ago, a2, b_r, b_l, rz2, rl2, rr2, rl1, rr1, zs, zr, ng,
    part, sib_part, up, ur, us, uin, so, ig, wg, gp, gsum,
    local_sem, a2a_s, a2a_r, p1_s, p1_r, p2_s, p2_r, agx_s, agx_r, ago_s, ago_r,
    rs_s, rs_r, sib_s, sib_r, up_s, up_r, gg_s, gg_r, out_sem,
):
    f32, bf16 = jnp.float32, jnp.bfloat16
    p = lax.axis_index("pipe")
    d = lax.axis_index("dp")
    c = lax.axis_index("tensor")
    xi, zh = d // 2, lax.rem(d, 2)
    o = 1 - c
    xr, xl, x2 = lax.rem(xi + 1, X), lax.rem(xi + 3, X), lax.rem(xi + 2, X)
    dz = xi * 2 + (1 - zh)
    dr, dl = xr * 2 + zh, xl * 2 + zh
    dx2, dx2z = x2 * 2 + zh, x2 * 2 + (1 - zh)
    drz, dlz = xr * 2 + (1 - zh), xl * 2 + (1 - zh)
    hc = xh.shape[-1]
    oc = gc.shape[-1]
    right, left, zdev = (p, dr, c), (p, dl, c), (p, dz, c)
    sib = (p, d, o)
    half_c = pl.ds(pl.multiple_of(c * hc, 128), hc)

    def pipe_peer(k):
        return lax.rem(p + k, 8)

    def dp_peer(k):
        return lax.rem(d + k, 8)

    sends = []

    def remote(src, dst, ssem, rsem, dev):
        cp = pltpu.make_async_remote_copy(
            src_ref=src, dst_ref=dst, send_sem=ssem, recv_sem=rsem,
            device_id=dev, device_id_type=MESH,
        )
        cp.start()
        sends.append(cp)
        return cp

    def landed(dst, rsem):
        pltpu.make_async_copy(dst, dst, rsem).wait()

    def local(src, dst, sem):
        cp = pltpu.make_async_copy(src, dst, sem)
        cp.start()
        return cp

    c_gown = local(
        grad_hbm.at[pl.ds(c * 64, 64), pl.ds(pl.multiple_of(d * oc, 128), oc)],
        gc.at[d, c], local_sem.at[6],
    )
    c_xf = local(x_hbm, xf, local_sem.at[0])
    c_xh = local(blocks_hbm.at[:, :, half_c], xh.at[pl.ds(0, 8)], local_sem.at[1])
    c_gain = local(gain_hbm.at[:, half_c], gain, local_sem.at[2])
    c_stage = local(parked_hbm.at[:, :, :, :, half_c], stage, local_sem.at[3])
    c_w = local(w_hbm, w, local_sem.at[4])
    c_gh = local(grad_hbm.at[:, half_c], gh, local_sem.at[5])
    later = []

    barrier = pltpu.get_barrier_semaphore()
    for k in range(1, 8):
        pl.semaphore_signal(barrier, inc=1, device_id=(pipe_peer(k), d, c), device_id_type=MESH)
        pl.semaphore_signal(barrier, inc=1, device_id=(p, dp_peer(k), c), device_id_type=MESH)
    pl.semaphore_signal(barrier, inc=1, device_id=sib, device_id_type=MESH)
    pl.semaphore_wait(barrier, 15)

    def cols(t):
        return pl.ds(pl.multiple_of(t * CT, CT), CT)

    n_t = hc // CT

    def loop(n):
        def run(body):
            def step(i, _):
                body(i)
                return 0

            lax.fori_loop(0, n, step, 0)

        return run

    def back(rows, t):
        return lax.dot_general(
            rows, w[cols(t), :], (((1,), (1,)), ((), ())), preferred_element_type=f32
        )

    def lanes(v):
        total = v[:, 0:128]
        for i in range(1, v.shape[1] // 128):
            total = total + v[:, i * 128:(i + 1) * 128]
        return total

    def place(hosts):
        h = [hosts[b] for b in range(8)]
        return [
            h[b] * 2 + sum([jnp.where(h[a] == h[b], 1, 0) for a in range(b)], jnp.int32(0))
            for b in range(8)
        ]

    def grads_out():
        for k in (2, 6, 1, 3, 5, 7, 4):
            q = dp_peer(k)
            remote(
                grad_hbm.at[pl.ds(c * 64, 64), pl.ds(pl.multiple_of(q * oc, 128), oc)],
                gc.at[d, c], a2a_s.at[k], a2a_r.at[k], (p, q, c),
            )

    def grads_sib():
        c_gown.wait()
        for k in range(1, 8):
            landed(gc.at[lax.rem(d + 8 - k, 8), c], a2a_r.at[k])
        remote(gc.at[:, c], gc.at[:, c], sib_s.at[0], sib_r.at[0], sib)

    def grads_in():
        c_w.wait()
        landed(gc.at[:, o], sib_r.at[0])

    def norm_new():
        c_xf.wait()
        c_xh.wait()
        c_gain.wait()

        @loop(8)
        def _(i):
            rows = pl.ds(pl.multiple_of(i * 16, 16), 16)
            v = xf[rows, :].astype(f32)
            scale = lax.rsqrt(jnp.mean(v * v, axis=-1, keepdims=True) + eps)
            val = (xh[i].astype(f32) * scale * gain[...]).astype(bf16)
            agx[d, i // 4, pl.ds(pl.multiple_of(lax.rem(i, 4) * 16, 16), 16), :] = val

    def own_z(buf, ss, rs):
        remote(buf.at[d], buf.at[d], ss.at[0], rs.at[0], zdev)

    def own_x(buf, ss, rs):
        remote(buf.at[d], buf.at[d], ss.at[1], rs.at[1], right)
        remote(buf.at[d], buf.at[d], ss.at[3], rs.at[3], left)

    def z_x(buf, ss, rs):
        landed(buf.at[dz], rs.at[0])
        remote(buf.at[dz], buf.at[dz], ss.at[2], rs.at[2], right)
        remote(buf.at[dz], buf.at[dz], ss.at[4], rs.at[4], left)

    def far_x(buf, ss, rs):
        landed(buf.at[dl], rs.at[1])
        remote(buf.at[dl, 0], buf.at[dl, 0], ss.at[5], rs.at[5], right)
        landed(buf.at[dr], rs.at[3])
        remote(buf.at[dr, 1], buf.at[dr, 1], ss.at[7], rs.at[7], left)

    def near_z(buf, rs):
        landed(buf.at[dlz], rs.at[2])
        landed(buf.at[drz], rs.at[4])

    def new_z():
        own_z(agx, agx_s, agx_r)

    def new_x():
        own_x(agx, agx_s, agx_r)

    def new_zx():
        z_x(agx, agx_s, agx_r)

    def new_far():
        far_x(agx, agx_s, agx_r)

    def new_far_z():
        landed(agx.at[dx2, 0], agx_r.at[5])
        remote(agx.at[dx2, 0], agx.at[dx2, 0], agx_s.at[6], agx_r.at[6], zdev)
        landed(agx.at[dx2, 1], agx_r.at[7])
        remote(agx.at[dx2, 1], agx.at[dx2, 1], agx_s.at[8], agx_r.at[8], zdev)

    def new_near():
        near_z(agx, agx_r)

    def stash_out():
        c_stage.wait()

        @loop(8)
        def _(s):
            p1s[s] = stage[jnp.maximum(flight[s] - 1, 0), s]

        for k in range(1, 8):
            q = pipe_peer(k)
            remote(p1s.at[q], p1r.at[pl.ds(p * 2, 2)], p1_s.at[k], p1_r.at[k], (q, d, c))
        later.append(local(p1s.at[p], p1r.at[pl.ds(p * 2, 2)], local_sem.at[7]))

    def norm_old():
        later.pop(0).wait()
        for k in range(1, 8):
            landed(p1r.at[pl.ds(lax.rem(p + 8 - k, 8) * 2, 2)], p1_r.at[k])
        old_at = place(hosts_old)
        for b in range(8):
            v = p1r[old_at[b]]
            early[pl.ds(b * 16, 16), :] = v
            v = v.astype(f32)
            part[0, pl.ds(b * 16, 16), :] = lanes(v * v)
        remote(part.at[0], sib_part.at[0], sib_s.at[1], sib_r.at[1], sib)
        landed(sib_part.at[0], sib_r.at[1])

        @loop(8)
        def _(i):
            rows = pl.ds(pl.multiple_of(i * 16, 16), 16)
            sq = jnp.sum(part[0, rows, :] + sib_part[0, rows, :], axis=-1, keepdims=True)
            scale = lax.rsqrt(sq / (2 * hc) + eps)
            oscale[rows, :] = jnp.broadcast_to(scale, (16, 128))
            val = (early[rows, :].astype(f32) * scale * gain[...]).astype(bf16)
            ago[d, i // 4, pl.ds(pl.multiple_of(lax.rem(i, 4) * 16, 16), 16), :] = val

    def old_z():
        own_z(ago, ago_s, ago_r)

    def old_x():
        own_x(ago, ago_s, ago_r)

    def old_zx():
        z_x(ago, ago_s, ago_r)

    def old_far():
        far_x(ago, ago_s, ago_r)

    def old_far_z():
        for h, n in ((0, 5), (1, 7)):
            landed(ago.at[dx2, h], ago_r.at[n])
            remote(
                ago.at[dx2, h, pl.ds(32, 32)], ago.at[dx2, h, pl.ds(32, 32)],
                ago_s.at[n + 4], ago_r.at[n + 4], zdev,
            )

    def old_far_x():
        near_z(ago, ago_r)
        for h, n, at, to in ((0, 6, dlz, right), (1, 8, drz, left)):
            remote(
                ago.at[at, h, pl.ds(0, 32)], ago.at[at, h, pl.ds(0, 32)],
                ago_s.at[n], ago_r.at[n], to,
            )

    def park_out():
        xh[8] = jnp.zeros((16, hc), bf16)
        new_at = place(hosts_new)
        for slot in range(16):
            which = 8 + sum([jnp.where(new_at[b] == slot, b - 8, 0) for b in range(8)], jnp.int32(0))
            p2s[slot // 2, slot % 2] = xh[which]
        for k in range(1, 8):
            q = pipe_peer(k)
            remote(p2s.at[q], p2r.at[p], p2_s.at[k], p2_r.at[k], (q, d, c))
        later.append(local(p2s.at[p], p2r.at[p], local_sem.at[8]))

    def park_sib():
        later.pop(0).wait()
        for k in range(1, 8):
            landed(p2r.at[lax.rem(p + 8 - k, 8)], p2_r.at[k])
        ends.append(local(p2r, pn_hbm.at[:, :, :, half_c], out_sem.at[6]))
        remote(p2r, pn_hbm.at[:, :, :, half_c], sib_s.at[2], sib_r.at[2], sib)

    def sum_far_z():
        @loop(n_t)
        def _(t):
            val = back(gc[dx2z].reshape(128, oc), t)
            a2[1, :, :, cols(t)] = val.astype(bf16).reshape(2, 64, CT)

        remote(a2.at[1], rz2, rs_s.at[0], rs_r.at[0], zdev)

    def sum_near_z():
        @loop(n_t)
        def _(t):
            val = back(gc[drz].reshape(128, oc), t)
            b_r[1 - zh, :, :, cols(t)] = val.astype(bf16).reshape(2, 64, CT)
            val = back(gc[dlz].reshape(128, oc), t)
            b_l[1 - zh, :, :, cols(t)] = val.astype(bf16).reshape(2, 64, CT)

        remote(b_r.at[1 - zh], rl1.at[1 - zh], rs_s.at[3], rs_r.at[3], right)
        remote(b_l.at[1 - zh], rr1.at[1 - zh], rs_s.at[4], rs_r.at[4], left)

    def sum_near():
        @loop(n_t)
        def _(t):
            b_r[zh, 1, :, cols(t)] = back(gc[dr, 1], t).astype(bf16)
            b_l[zh, 0, :, cols(t)] = back(gc[dl, 0], t).astype(bf16)

        remote(b_r.at[zh, 1], rl1.at[zh, 1], rs_s.at[5], rs_r.at[5], right)
        remote(b_l.at[zh, 0], rr1.at[zh, 0], rs_s.at[6], rs_r.at[6], left)

    def sum_far():
        landed(rz2, rs_r.at[0])

        @loop(n_t)
        def _(t):
            val = back(gc[dx2].reshape(128, oc), t)
            val = val + rz2[:, :, cols(t)].reshape(128, CT).astype(f32)
            a2[0, :, :, cols(t)] = val.astype(bf16).reshape(2, 64, CT)

        remote(a2.at[0, 0], rl2, rs_s.at[1], rs_r.at[1], right)
        remote(a2.at[0, 1], rr2, rs_s.at[2], rs_r.at[2], left)

    def sum_through():
        landed(rl2, rs_r.at[1])
        landed(rr2, rs_r.at[2])

        @loop(n_t)
        def _(t):
            val = back(gc[dr, 0], t) + rl2[:, cols(t)].astype(f32)
            b_r[zh, 0, :, cols(t)] = val.astype(bf16)
            val = back(gc[dl, 1], t) + rr2[:, cols(t)].astype(f32)
            b_l[zh, 1, :, cols(t)] = val.astype(bf16)

        remote(b_r.at[zh, 0], rl1.at[zh, 0], rs_s.at[7], rs_r.at[7], right)
        remote(b_l.at[zh, 1], rr1.at[zh, 1], rs_s.at[8], rs_r.at[8], left)

    def sum_z():
        landed(rl1.at[1 - zh], rs_r.at[3])
        landed(rr1.at[1 - zh], rs_r.at[4])

        @loop(n_t)
        def _(t):
            val = back(gc[dz].reshape(128, oc), t)
            val = val + rl1[1 - zh, :, :, cols(t)].reshape(128, CT).astype(f32)
            val = val + rr1[1 - zh, :, :, cols(t)].reshape(128, CT).astype(f32)
            zs[:, cols(t)] = val.astype(bf16)

        remote(zs, zr, rs_s.at[9], rs_r.at[9], zdev)

    def sum_own():
        landed(rl1.at[zh, 1], rs_r.at[5])
        landed(rr1.at[zh, 0], rs_r.at[6])
        landed(rl1.at[zh, 0], rs_r.at[7])
        landed(rr1.at[zh, 1], rs_r.at[8])
        landed(zr, rs_r.at[9])
        part[1] = jnp.zeros((128, 128), f32)

        @loop(n_t)
        def _(t):
            val = back(gc[d].reshape(128, oc), t)
            val = val + rl1[zh, :, :, cols(t)].reshape(128, CT).astype(f32)
            val = val + rr1[zh, :, :, cols(t)].reshape(128, CT).astype(f32)
            val = val + zr[:, cols(t)].astype(f32)
            ng[:, cols(t)] = val
            term = val * (early[:, cols(t)].astype(f32) * oscale[:, 0:1])
            gp[d, :, cols(t)] = jnp.sum(term, axis=0, keepdims=True)
            part[1] = part[1] + lanes(term * gain[:, cols(t)])

        remote(part.at[1], sib_part.at[1], sib_s.at[3], sib_r.at[3], sib)
        for k in range(1, 8):
            remote(gp.at[d], gp.at[d], gg_s.at[k], gg_r.at[k], (p, dp_peer(k), c))

    def project(xq, i):
        two = pl.ds(xq * 2, 2)

        @loop(n_t)
        def _(t):
            val = jnp.dot(
                agx[two, :, :, cols(t)].reshape(256, CT), w[cols(t), :],
                preferred_element_type=f32,
            ).reshape(2, 2, 64, oc)

            @pl.when(t == 0)
            def _():
                up[two] = val

            @pl.when(t > 0)
            def _():
                up[two] = up[two] + val

        remote(up.at[two, o], ur.at[two], up_s.at[i], up_r.at[i], sib)

    def project_sum(xq, i):
        two = pl.ds(xq * 2, 2)
        landed(ur.at[two], up_r.at[i])
        us[two] = (up[two, c] + ur[two]).astype(bf16)

    def project_near():
        project(xi, 0)
        project(xl, 1)
        project(xr, 2)

    def update_near():
        project_sum(xi, 0)
        project_sum(xl, 1)
        project_sum(xr, 2)
        uin[d] = us[d]
        remote(us.at[dz], uin.at[d], up_s.at[4], up_r.at[4], zdev)
        remote(us.at[dl], uin.at[d], up_s.at[5], up_r.at[5], left)
        remote(us.at[dr], uin.at[d], up_s.at[6], up_r.at[6], right)
        remote(us.at[dlz], uin.at[d], up_s.at[7], up_r.at[7], (p, dlz, c))
        remote(us.at[drz], uin.at[d], up_s.at[8], up_r.at[8], (p, drz, c))

    def update_far():
        landed(agx.at[dx2z, 0], agx_r.at[6])
        landed(agx.at[dx2z, 1], agx_r.at[8])
        project(x2, 3)
        project_sum(x2, 3)
        remote(us.at[dx2], uin.at[d], up_s.at[9], up_r.at[9], (p, dx2, c))
        remote(us.at[dx2z], uin.at[d], up_s.at[10], up_r.at[10], (p, dx2z, c))

    mine = pl.ds(pl.multiple_of(c * 64, 64), 64)

    def output():
        for k, at in ((4, dz), (5, dr), (6, dl), (7, drz), (8, dlz), (9, dx2), (10, dx2z)):
            landed(uin.at[at], up_r.at[k])

        @loop(8)
        def _(q):
            at = pl.ds(pl.multiple_of(q * oc, 128), oc)
            so[:, at] = (xf[mine, at].astype(f32) + uin[q].astype(f32)).astype(bf16)

        ends.append(local(so, so_hbm.at[mine, :], out_sem.at[0]))
        remote(so, so_hbm.at[mine, :], sib_s.at[4], sib_r.at[4], sib)

    def input_out():
        landed(sib_part.at[1], sib_r.at[3])
        c_gh.wait()

        @loop(8)
        def _(i):
            rows = pl.ds(pl.multiple_of(i * 16, 16), 16)
            mean = jnp.sum(part[1, rows, :] + sib_part[1, rows, :], axis=-1, keepdims=True) / (2 * hc)
            scale = oscale[rows, 0:1]
            old_hat = early[rows, :].astype(f32) * scale
            centred = ng[rows, :] * gain[...] - old_hat * mean
            ig[rows, :] = (gh[rows, :].astype(f32) + scale * centred).astype(bf16)

        ends.append(local(ig, ig_hbm.at[:, half_c], out_sem.at[1]))
        remote(ig, ig_hbm.at[:, half_c], sib_s.at[5], sib_r.at[5], sib)

    def gain_out():
        for k in range(1, 8):
            landed(gp.at[0], gg_r.at[k])
        total = gp[0]
        for q in range(1, 8):
            total = total + gp[q]
        gsum[...] = total
        ends.append(local(gsum, gg_hbm.at[:, half_c], out_sem.at[2]))
        remote(gsum, gg_hbm.at[:, half_c], sib_s.at[6], sib_r.at[6], sib)

    def weight_part(xq, first):
        two = pl.ds(xq * 2, 2)

        @loop(n_t)
        def _(t):
            val = lax.dot_general(
                ago[two, :, :, cols(t)].reshape(256, CT), gc[two].reshape(256, oc),
                (((0,), (0,)), ((), ())), preferred_element_type=f32,
            )
            if first:
                wg[cols(t), :] = val
            else:
                wg[cols(t), :] = wg[cols(t), :] + val

    def weight_own():
        weight_part(xi, True)

    def weight_near():
        weight_part(xl, False)
        weight_part(xr, False)
        ends.append(local(wg, wg_hbm, out_sem.at[3]))
        ends.append(local(gc.at[pl.ds(x2 * 2, 2)], gc2_hbm, out_sem.at[4]))

    def weight_rows():
        for n in (6, 8, 9, 11):
            landed(ago.at[dx2z, 0, pl.ds(0, 32)], ago_r.at[n])
        ends.append(local(ago.at[pl.ds(x2 * 2, 2)], ago2_hbm, out_sem.at[5]))

    ends = []
    for step in (
        grads_out, norm_new, stash_out, new_x, grads_sib, new_z, grads_in, sum_far_z,
        sum_near_z, new_far, sum_near, new_zx, new_far_z, park_out, sum_far, norm_old,
        sum_through, new_near, old_x, old_z, project_near, park_sib, update_far, old_far,
        old_zx, weight_own, sum_z, update_near, sum_own, old_far_z, input_out, output,
        old_far_x, weight_near, gain_out, weight_rows,
    ):
        step()

    half_o = pl.ds(pl.multiple_of(o * hc, 128), hc)
    landed(pn_hbm.at[:, :, :, half_o], sib_r.at[2])
    landed(so_hbm.at[pl.ds(pl.multiple_of(o * 64, 64), 64), :], sib_r.at[4])
    landed(ig_hbm.at[:, half_o], sib_r.at[5])
    landed(gg_hbm.at[:, half_o], sib_r.at[6])
    for cp in ends:
        cp.wait()
    for cp in sends:
        cp.wait_send()


def finish(
    so_in, ig_in, gg_in, pn_in, part, rows, grads, so, ig, gg, pn, wg,
    v_so, v_ig, v_gg, v_pn, v_wg, v_rows, v_grads, in_sem, out_sem,
):
    tiles = [pl.ds(t * CT, CT) for t in range(part.shape[0] // CT)]
    halves = [pl.ds(i * 4, 4) for i in range(2)]
    moves = [(part.at[t], v_wg.at[t], wg.at[t]) for t in tiles]
    plain = [(so_in, v_so, so), (ig_in, v_ig, ig), (gg_in, v_gg, gg)]
    plain += [(pn_in.at[h], v_pn.at[h], pn.at[h]) for h in halves]
    order = []
    for i in range(len(tiles)):
        order += [(i, moves[i]), (len(tiles) + i, plain[i])]

    def copy(src, dst, sem):
        cp = pltpu.make_async_copy(src, dst, sem)
        cp.start()
        return cp

    first = [copy(rows, v_rows, in_sem.at[10]), copy(grads, v_grads, in_sem.at[11])]
    loads = [copy(src, mid, in_sem.at[i]) for i, (src, mid, _) in order]
    for cp in first:
        cp.wait()
    stores = []
    for (i, (_, mid, dst)), load in zip(order, loads):
        load.wait()
        if i < len(tiles):
            mid[...] = mid[...] + lax.dot_general(
                v_rows[:, tiles[i]], v_grads[...], (((0,), (0,)), ((), ())),
                preferred_element_type=jnp.float32,
            )
        stores.append(copy(mid, dst, out_sem.at[i]))
    for cp in stores:
        cp.wait()


def local(section_inputs, output_grad, norm_gain, weight, parked, in_flight, old_hosts, new_hosts):
    rows, width = section_inputs.shape[1:]
    hc, oc = weight.shape[1:]
    f32, bf16 = jnp.float32, jnp.bfloat16
    hbm = pl.BlockSpec(memory_space=pl.ANY)
    smem = pl.BlockSpec(memory_space=pltpu.SMEM)
    vm = pltpu.VMEM
    dma = pltpu.SemaphoreType.DMA
    so_p, ig_p, wg_p, gg_p, pn_p, rows_p, grads_p = pl.pallas_call(
        kernel,
        out_shape=(
            jax.ShapeDtypeStruct((rows, width), bf16),
            jax.ShapeDtypeStruct((rows, width), bf16),
            jax.ShapeDtypeStruct((hc, oc), f32),
            jax.ShapeDtypeStruct((1, width), f32),
            jax.ShapeDtypeStruct((8, 2, 16, width), bf16),
            jax.ShapeDtypeStruct((2, 2, 64, hc), bf16),
            jax.ShapeDtypeStruct((2, 2, 64, oc), bf16),
        ),
        in_specs=[hbm] * 6 + [smem] * 3,
        out_specs=(hbm,) * 7,
        scratch_shapes=[
            vm((rows, width), bf16),
            vm((9, 16, hc), bf16),
            vm((rows, hc), bf16),
            vm((1, hc), f32),
            vm((hc, oc), bf16),
            vm((3, 8, 2, 16, hc), bf16),
            vm((8, 2, 16, hc), bf16),
            vm((16, 16, hc), bf16),
            vm((rows, hc), bf16),
            vm((rows, 128), f32),
            vm((8, 2, 16, hc), bf16),
            vm((8, 2, 16, hc), bf16),
            vm((8, 2, 64, oc), bf16),
            vm((8, 2, 64, hc), bf16),
            vm((8, 2, 64, hc), bf16),
            vm((2, 2, 64, hc), bf16),
            vm((2, 2, 64, hc), bf16),
            vm((2, 2, 64, hc), bf16),
            vm((2, 64, hc), bf16),
            vm((64, hc), bf16),
            vm((64, hc), bf16),
            vm((2, 2, 64, hc), bf16),
            vm((2, 2, 64, hc), bf16),
            vm((rows, hc), bf16),
            vm((rows, hc), bf16),
            vm((rows, hc), f32),
            vm((2, rows, 128), f32),
            vm((2, rows, 128), f32),
            vm((8, 2, 64, oc), f32),
            vm((8, 64, oc), f32),
            vm((8, 64, oc), bf16),
            vm((8, 64, oc), bf16),
            vm((64, width), bf16),
            vm((rows, hc), bf16),
            vm((hc, oc), f32),
            vm((8, 1, hc), f32),
            vm((1, hc), f32),
            dma((9,)),
            dma((8,)), dma((8,)),
            dma((8,)), dma((8,)),
            dma((8,)), dma((8,)),
            dma((9,)), dma((9,)),
            dma((12,)), dma((12,)),
            dma((10,)), dma((10,)),
            dma((7,)), dma((7,)),
            dma((11,)), dma((11,)),
            dma((8,)), dma((8,)),
            dma((7,)),
        ],
        compiler_params=pltpu.CompilerParams(
            collective_id=0, has_side_effects=True, vmem_limit_bytes=62 * 2**20
        ),
        cost_estimate=pl.CostEstimate(flops=10 * 2**30, bytes_accessed=40 * 2**20, transcendentals=0),
        name="relay_step",
    )(
        section_inputs[0], section_inputs[0].reshape(8, 16, width), output_grad[0], norm_gain, weight[0], parked[0],
        in_flight, old_hosts[0, :, 0], new_hosts[0, :, 0],
    )
    so, ig, gg, pn, wg = pl.pallas_call(
        finish,
        out_shape=(
            jax.ShapeDtypeStruct((rows, width), bf16),
            jax.ShapeDtypeStruct((rows, width), bf16),
            jax.ShapeDtypeStruct((1, width), f32),
            jax.ShapeDtypeStruct((8, 2, 16, width), bf16),
            jax.ShapeDtypeStruct((hc, oc), f32),
        ),
        in_specs=[hbm] * 7,
        out_specs=[hbm] * 5,
        scratch_shapes=[
            vm((rows, width), bf16),
            vm((rows, width), bf16),
            vm((1, width), f32),
            vm((8, 2, 16, width), bf16),
            vm((hc, oc), f32),
            vm((256, hc), bf16),
            vm((256, oc), bf16),
            dma((12,)),
            dma((10,)),
        ],
        compiler_params=pltpu.CompilerParams(vmem_limit_bytes=62 * 2**20),
        cost_estimate=pl.CostEstimate(flops=2**30, bytes_accessed=25 * 2**20, transcendentals=0),
        name="finish",
    )(so_p, ig_p, gg_p, pn_p, wg_p, rows_p.reshape(256, hc), grads_p.reshape(256, oc))
    return so[None], ig[None], wg[None], gg, pn[None]


def solution(mesh):
    in_specs = (
        P("pipe", "dp", None),
        P("pipe", "dp", None),
        P("pipe", None),
        P("pipe", "tensor", "dp"),
        P("pipe", None, None, "dp", None, None),
        P(),
        P("pipe", "dp", None),
        P("pipe", "dp", None),
    )
    out_specs = (
        P("pipe", "dp", None),
        P("pipe", "dp", None),
        P("pipe", "tensor", "dp"),
        P("pipe", None),
        P("pipe", None, "dp", None, None),
    )
    return jax.shard_map(local, mesh=mesh, in_specs=in_specs, out_specs=out_specs, check_vma=False)
```

time: 453 us -> 162 us (0.36)
  waiting for transfers between devices: 228 us -> 0 us
  Pallas kernels: 0 us -> 160 us
  blocking collectives: 122 us -> 0 us
  other arithmetic: 27.8 us -> 0 us
  matrix products: 26.3 us -> 0 us
  local copies, waits for them, and re-layouts: 22.6 us -> 0 us
  between operations: 13.9 us -> 0.64 us
  starting transfers between devices: 9.5 us -> 0 us
    pallas_call x0 -> x2, Pallas kernels: none -> 160 us  [the longest x1 151 us: local(): pl.pallas_call(kernel, out_shape=(jax.ShapeDtypeStruct((rows, width), bf1...]
    reduce_scatter x1 -> x0, waiting for transfers between devices: 148 us -> none  [local(): lax.psum_scatter(lax.dot_general(grad_cols, w_local, (((1,), (1,)), ((),...]
    all_gather x3 -> x0, waiting for transfers between devices: 79.8 us -> none  [the longest x1 60.4 us: local(): lax.all_gather(normed_half, 'dp', axis=0, tiled=True)]
    all_to_all x2 -> x0, blocking collectives: 67.4 us -> none  [the longest x1 41.9 us: local(): lax.all_to_all(placed.reshape(sections, capacity, rows_block, width), 'pi...]
    psum x2 -> x0, blocking collectives: 54.9 us -> none  [the longest x1 42.5 us: local(): gain_grad = lax.psum(gain_term, 'dp')]
    dot_general x3 -> x0, matrix products: 26.3 us -> none  [the longest x1 9.96 us: local(): lax.dot_general(lax.all_gather(old_half, 'dp', axis=0, tiled=True), grad_...]
    reduce_sum x6 -> x0, other arithmetic: 14.7 us -> none  [the longest x1 7.59 us: local(): jnp.sum(jnp.where(picked[:, :, None, None, None], stash, jnp.zeros((), st...]
    convert_element_type x4 -> x0, other arithmetic: 9.44 us -> none  [the longest x1 3.57 us: local(): (input_batch.astype(jnp.float32) + update.astype(jnp.float32)).astype(jnp...]
  transfers between devices with their start and end apart: 6 -> 0, of which waited for: 4 -> 0; matrix products, arithmetic and copies ran while one was open for 10% -> 0% of each run, Pallas kernels for 0% -> 0%
where the time goes in v2:
time: 162 us; the launch traced here: 161 us
  Pallas kernels  160 us (99%)
    pallas_call x1, Pallas kernels, local(): pl.pallas_call(kernel, out_shape=(jax.ShapeDtypeStruct((rows, width), bf1...  151 us
    pallas_call x1, Pallas kernels, local(): pl.pallas_call(finish, out_shape=(jax.ShapeDtypeStruct((rows, width), bf1...  9.45 us

profile of v2, /device:TPU:9, one launch (start us, length us, event | category | flops | bytes accessed | tf_op | source)
XLA Modules:
  0.0 160.7 jit_solution(5981246257131593637)
XLA Ops:
  0.6 150.6 %relay_step.1 = (bf16[128,5120]{1,0:T(8,128)(2,1)}, bf16[128,5120]{1,0:T(8,128)(2,1)}, f32[2560,640]{1,0:T(8,128)}, f32[1,5120]{1,0:T(1,128)}, bf16[8,2,16,5120]...) custom-call(bf16[128,5120]{1,0:T(8,128)(2,1)} %bitcast.19, ...), custom_call_target="tpu_custom_call" | custom-call | flops 10737418240 | bytes 41943040 | tf_op jit(solution)/shard_map/relay_step/pallas_call | solution.py:544
  151.3 9.5 %finish.1 = (bf16[128,5120]{1,0:T(8,128)(2,1)}, bf16[128,5120]{1,0:T(8,128)(2,1)}, f32[1,5120]{1,0:T(1,128)}, bf16[8,2,16,5120]{3,2,1,0:T(8,128)(2,1)}, f32[2560,640]{1,0:T(8,128)}) custom-call(bf16[128,5120]{1,0:T(8,128)(2,1)} %get-tuple-element.17.so_in, bf16[128,5120]{1,0:T(8,128)(2,1)} %get-tuple-element.18.ig_in, f32[1,5120]{1,0:T(1,128)} %get-tuple-element.19.gg_in, ...), custom_call_target="tpu_custom_call" | custom-call | flops 1073741824 | bytes 26214400 | tf_op jit(solution)/shard_map/finish/pallas_call | solution.py:616

commit v3 on v2

--- a/solution.py
+++ b/solution.py
@@ -10,6 +10,7 @@
 eps = 1e-05
 MESH = pl.DeviceIdType.MESH
 X = 4
+OWN, RIGHT, LEFT, FAR = 0, 2, 4, 6
 CT = 512
 
 
@@ -17,7 +18,7 @@
     x_hbm, blocks_hbm, grad_hbm, gain_hbm, w_hbm, parked_hbm, flight, hosts_old, hosts_new,
     so_hbm, ig_hbm, wg_hbm, gg_hbm, pn_hbm, ago2_hbm, gc2_hbm,
     xf, xh, gh, gain, w, stage, p1s, p1r, early, oscale, p2s, p2r, gc,
-    agx, ago, a2, b_r, b_l, rz2, rl2, rr2, rl1, rr1, zs, zr, ng,
+    agx, ago, a2, b_r, b_l, rz2, rl2, rr2, rl1, rr1, zs, zr, sums, ng,
     part, sib_part, up, ur, us, uin, so, ig, wg, gp, gsum,
     local_sem, a2a_s, a2a_r, p1_s, p1_r, p2_s, p2_r, agx_s, agx_r, ago_s, ago_r,
     rs_s, rs_r, sib_s, sib_r, up_s, up_r, gg_s, gg_r, out_sem,
@@ -66,7 +67,7 @@
 
     c_gown = local(
         grad_hbm.at[pl.ds(c * 64, 64), pl.ds(pl.multiple_of(d * oc, 128), oc)],
-        gc.at[d, c], local_sem.at[6],
+        gc.at[OWN, c], local_sem.at[6],
     )
     c_xf = local(x_hbm, xf, local_sem.at[0])
     c_xh = local(blocks_hbm.at[:, :, half_c], xh.at[pl.ds(0, 8)], local_sem.at[1])
@@ -116,18 +117,21 @@
             for b in range(8)
         ]
 
+    peers = [d, dz, dr, drz, dl, dlz, dx2, dx2z]
+    there = [0, 1, 4, 5, 2, 3, 6, 7]
+
     def grads_out():
-        for k in (2, 6, 1, 3, 5, 7, 4):
-            q = dp_peer(k)
+        for k in (1, 2, 4, 6, 3, 5, 7):
+            q = peers[k]
             remote(
                 grad_hbm.at[pl.ds(c * 64, 64), pl.ds(pl.multiple_of(q * oc, 128), oc)],
-                gc.at[d, c], a2a_s.at[k], a2a_r.at[k], (p, q, c),
+                gc.at[there[k], c], a2a_s.at[k], a2a_r.at[there[k]], (p, q, c),
             )
 
     def grads_sib():
         c_gown.wait()
         for k in range(1, 8):
-            landed(gc.at[lax.rem(d + 8 - k, 8), c], a2a_r.at[k])
+            landed(gc.at[k, c], a2a_r.at[k])
         remote(gc.at[:, c], gc.at[:, c], sib_s.at[0], sib_r.at[0], sib)
 
     def grads_in():
@@ -145,29 +149,29 @@
             v = xf[rows, :].astype(f32)
             scale = lax.rsqrt(jnp.mean(v * v, axis=-1, keepdims=True) + eps)
             val = (xh[i].astype(f32) * scale * gain[...]).astype(bf16)
-            agx[d, i // 4, pl.ds(pl.multiple_of(lax.rem(i, 4) * 16, 16), 16), :] = val
+            agx[OWN, i // 4, pl.ds(pl.multiple_of(lax.rem(i, 4) * 16, 16), 16), :] = val
 
     def own_z(buf, ss, rs):
-        remote(buf.at[d], buf.at[d], ss.at[0], rs.at[0], zdev)
+        remote(buf.at[OWN], buf.at[OWN + 1], ss.at[0], rs.at[0], zdev)
 
     def own_x(buf, ss, rs):
-        remote(buf.at[d], buf.at[d], ss.at[1], rs.at[1], right)
-        remote(buf.at[d], buf.at[d], ss.at[3], rs.at[3], left)
+        remote(buf.at[OWN], buf.at[LEFT], ss.at[1], rs.at[1], right)
+        remote(buf.at[OWN], buf.at[RIGHT], ss.at[3], rs.at[3], left)
 
     def z_x(buf, ss, rs):
-        landed(buf.at[dz], rs.at[0])
-        remote(buf.at[dz], buf.at[dz], ss.at[2], rs.at[2], right)
-        remote(buf.at[dz], buf.at[dz], ss.at[4], rs.at[4], left)
+        landed(buf.at[OWN + 1], rs.at[0])
+        remote(buf.at[OWN + 1], buf.at[LEFT + 1], ss.at[2], rs.at[2], right)
+        remote(buf.at[OWN + 1], buf.at[RIGHT + 1], ss.at[4], rs.at[4], left)
 
     def far_x(buf, ss, rs):
-        landed(buf.at[dl], rs.at[1])
-        remote(buf.at[dl, 0], buf.at[dl, 0], ss.at[5], rs.at[5], right)
-        landed(buf.at[dr], rs.at[3])
-        remote(buf.at[dr, 1], buf.at[dr, 1], ss.at[7], rs.at[7], left)
+        landed(buf.at[LEFT], rs.at[1])
+        remote(buf.at[LEFT, 0], buf.at[FAR, 0], ss.at[5], rs.at[5], right)
+        landed(buf.at[RIGHT], rs.at[3])
+        remote(buf.at[RIGHT, 1], buf.at[FAR, 1], ss.at[7], rs.at[7], left)
 
     def near_z(buf, rs):
-        landed(buf.at[dlz], rs.at[2])
-        landed(buf.at[drz], rs.at[4])
+        landed(buf.at[LEFT + 1], rs.at[2])
+        landed(buf.at[RIGHT + 1], rs.at[4])
 
     def new_z():
         own_z(agx, agx_s, agx_r)
@@ -182,10 +186,9 @@
         far_x(agx, agx_s, agx_r)
 
     def new_far_z():
-        landed(agx.at[dx2, 0], agx_r.at[5])
-        remote(agx.at[dx2, 0], agx.at[dx2, 0], agx_s.at[6], agx_r.at[6], zdev)
-        landed(agx.at[dx2, 1], agx_r.at[7])
-        remote(agx.at[dx2, 1], agx.at[dx2, 1], agx_s.at[8], agx_r.at[8], zdev)
+        for h, n in ((0, 5), (1, 7)):
+            landed(agx.at[FAR, h], agx_r.at[n])
+            remote(agx.at[FAR, h], agx.at[FAR + 1, h], agx_s.at[n + 1], agx_r.at[n + 1], zdev)
 
     def new_near():
         near_z(agx, agx_r)
@@ -222,7 +225,7 @@
             scale = lax.rsqrt(sq / (2 * hc) + eps)
             oscale[rows, :] = jnp.broadcast_to(scale, (16, 128))
             val = (early[rows, :].astype(f32) * scale * gain[...]).astype(bf16)
-            ago[d, i // 4, pl.ds(pl.multiple_of(lax.rem(i, 4) * 16, 16), 16), :] = val
+            ago[OWN, i // 4, pl.ds(pl.multiple_of(lax.rem(i, 4) * 16, 16), 16), :] = val
 
     def old_z():
         own_z(ago, ago_s, ago_r)
@@ -238,17 +241,17 @@
 
     def old_far_z():
         for h, n in ((0, 5), (1, 7)):
-            landed(ago.at[dx2, h], ago_r.at[n])
+            landed(ago.at[FAR, h], ago_r.at[n])
             remote(
-                ago.at[dx2, h, pl.ds(32, 32)], ago.at[dx2, h, pl.ds(32, 32)],
+                ago.at[FAR, h, pl.ds(32, 32)], ago.at[FAR + 1, h, pl.ds(32, 32)],
                 ago_s.at[n + 4], ago_r.at[n + 4], zdev,
             )
 
     def old_far_x():
         near_z(ago, ago_r)
-        for h, n, at, to in ((0, 6, dlz, right), (1, 8, drz, left)):
+        for h, n, at, to in ((0, 6, LEFT + 1, right), (1, 8, RIGHT + 1, left)):
             remote(
-                ago.at[at, h, pl.ds(0, 32)], ago.at[at, h, pl.ds(0, 32)],
+                ago.at[at, h, pl.ds(0, 32)], ago.at[FAR + 1, h, pl.ds(0, 32)],
                 ago_s.at[n], ago_r.at[n], to,
             )
 
@@ -270,42 +273,37 @@
         ends.append(local(p2r, pn_hbm.at[:, :, :, half_c], out_sem.at[6]))
         remote(p2r, pn_hbm.at[:, :, :, half_c], sib_s.at[2], sib_r.at[2], sib)
 
-    def sum_far_z():
+    def sum_first():
         @loop(n_t)
         def _(t):
-            val = back(gc[dx2z].reshape(128, oc), t)
-            a2[1, :, :, cols(t)] = val.astype(bf16).reshape(2, 64, CT)
+            val = back(gc[...].reshape(1024, oc), t).reshape(8, 2, 64, CT)
+            a2[1, :, :, cols(t)] = val[FAR + 1].astype(bf16)
+            b_r[1, :, :, cols(t)] = val[RIGHT + 1].astype(bf16)
+            b_l[1, :, :, cols(t)] = val[LEFT + 1].astype(bf16)
+            b_r[0, 1, :, cols(t)] = val[RIGHT, 1].astype(bf16)
+            b_l[0, 0, :, cols(t)] = val[LEFT, 0].astype(bf16)
+            sums[0, :, :, cols(t)] = val[FAR]
+            sums[1, 0, :, cols(t)] = val[RIGHT, 0]
+            sums[1, 1, :, cols(t)] = val[LEFT, 1]
+            sums[2, :, :, cols(t)] = val[OWN + 1]
+            sums[3, :, :, cols(t)] = val[OWN]
 
         remote(a2.at[1], rz2, rs_s.at[0], rs_r.at[0], zdev)
 
     def sum_near_z():
+        remote(b_r.at[1], rl1.at[1], rs_s.at[3], rs_r.at[3], right)
+        remote(b_l.at[1], rr1.at[1], rs_s.at[4], rs_r.at[4], left)
+
+    def sum_near():
+        remote(b_r.at[0, 1], rl1.at[0, 1], rs_s.at[5], rs_r.at[5], right)
+        remote(b_l.at[0, 0], rr1.at[0, 0], rs_s.at[6], rs_r.at[6], left)
+
+    def sum_far():
+        landed(rz2, rs_r.at[0])
+
         @loop(n_t)
         def _(t):
-            val = back(gc[drz].reshape(128, oc), t)
-            b_r[1 - zh, :, :, cols(t)] = val.astype(bf16).reshape(2, 64, CT)
-            val = back(gc[dlz].reshape(128, oc), t)
-            b_l[1 - zh, :, :, cols(t)] = val.astype(bf16).reshape(2, 64, CT)
-
-        remote(b_r.at[1 - zh], rl1.at[1 - zh], rs_s.at[3], rs_r.at[3], right)
-        remote(b_l.at[1 - zh], rr1.at[1 - zh], rs_s.at[4], rs_r.at[4], left)
-
-    def sum_near():
-        @loop(n_t)
-        def _(t):
-            b_r[zh, 1, :, cols(t)] = back(gc[dr, 1], t).astype(bf16)
-            b_l[zh, 0, :, cols(t)] = back(gc[dl, 0], t).astype(bf16)
-
-        remote(b_r.at[zh, 1], rl1.at[zh, 1], rs_s.at[5], rs_r.at[5], right)
-        remote(b_l.at[zh, 0], rr1.at[zh, 0], rs_s.at[6], rs_r.at[6], left)
-
-    def sum_far():
-        landed(rz2, rs_r.at[0])
-
-        @loop(n_t)
-        def _(t):
-            val = back(gc[dx2].reshape(128, oc), t)
-            val = val + rz2[:, :, cols(t)].reshape(128, CT).astype(f32)
-            a2[0, :, :, cols(t)] = val.astype(bf16).reshape(2, 64, CT)
+            a2[0, :, :, cols(t)] = (sums[0, :, :, cols(t)] + rz2[:, :, cols(t)].astype(f32)).astype(bf16)
 
         remote(a2.at[0, 0], rl2, rs_s.at[1], rs_r.at[1], right)
         remote(a2.at[0, 1], rr2, rs_s.at[2], rs_r.at[2], left)
@@ -316,41 +314,37 @@
 
         @loop(n_t)
         def _(t):
-            val = back(gc[dr, 0], t) + rl2[:, cols(t)].astype(f32)
-            b_r[zh, 0, :, cols(t)] = val.astype(bf16)
-            val = back(gc[dl, 1], t) + rr2[:, cols(t)].astype(f32)
-            b_l[zh, 1, :, cols(t)] = val.astype(bf16)
-
-        remote(b_r.at[zh, 0], rl1.at[zh, 0], rs_s.at[7], rs_r.at[7], right)
-        remote(b_l.at[zh, 1], rr1.at[zh, 1], rs_s.at[8], rs_r.at[8], left)
+            b_r[0, 0, :, cols(t)] = (sums[1, 0, :, cols(t)] + rl2[:, cols(t)].astype(f32)).astype(bf16)
+            b_l[0, 1, :, cols(t)] = (sums[1, 1, :, cols(t)] + rr2[:, cols(t)].astype(f32)).astype(bf16)
+
+        remote(b_r.at[0, 0], rl1.at[0, 0], rs_s.at[7], rs_r.at[7], right)
+        remote(b_l.at[0, 1], rr1.at[0, 1], rs_s.at[8], rs_r.at[8], left)
 
     def sum_z():
-        landed(rl1.at[1 - zh], rs_r.at[3])
-        landed(rr1.at[1 - zh], rs_r.at[4])
+        landed(rl1.at[1], rs_r.at[3])
+        landed(rr1.at[1], rs_r.at[4])
 
         @loop(n_t)
         def _(t):
-            val = back(gc[dz].reshape(128, oc), t)
-            val = val + rl1[1 - zh, :, :, cols(t)].reshape(128, CT).astype(f32)
-            val = val + rr1[1 - zh, :, :, cols(t)].reshape(128, CT).astype(f32)
-            zs[:, cols(t)] = val.astype(bf16)
+            val = sums[2, :, :, cols(t)] + rl1[1, :, :, cols(t)].astype(f32)
+            val = val + rr1[1, :, :, cols(t)].astype(f32)
+            zs[:, cols(t)] = val.astype(bf16).reshape(128, CT)
 
         remote(zs, zr, rs_s.at[9], rs_r.at[9], zdev)
 
     def sum_own():
-        landed(rl1.at[zh, 1], rs_r.at[5])
-        landed(rr1.at[zh, 0], rs_r.at[6])
-        landed(rl1.at[zh, 0], rs_r.at[7])
-        landed(rr1.at[zh, 1], rs_r.at[8])
+        landed(rl1.at[0, 1], rs_r.at[5])
+        landed(rr1.at[0, 0], rs_r.at[6])
+        landed(rl1.at[0, 0], rs_r.at[7])
+        landed(rr1.at[0, 1], rs_r.at[8])
         landed(zr, rs_r.at[9])
         part[1] = jnp.zeros((128, 128), f32)
 
         @loop(n_t)
         def _(t):
-            val = back(gc[d].reshape(128, oc), t)
-            val = val + rl1[zh, :, :, cols(t)].reshape(128, CT).astype(f32)
-            val = val + rr1[zh, :, :, cols(t)].reshape(128, CT).astype(f32)
-            val = val + zr[:, cols(t)].astype(f32)
+            val = sums[3, :, :, cols(t)] + rl1[0, :, :, cols(t)].astype(f32)
+            val = val + rr1[0, :, :, cols(t)].astype(f32)
+            val = val.reshape(128, CT) + zr[:, cols(t)].astype(f32)
             ng[:, cols(t)] = val
             term = val * (early[:, cols(t)].astype(f32) * oscale[:, 0:1])
             gp[d, :, cols(t)] = jnp.sum(term, axis=0, keepdims=True)
@@ -360,8 +354,8 @@
         for k in range(1, 8):
             remote(gp.at[d], gp.at[d], gg_s.at[k], gg_r.at[k], (p, dp_peer(k), c))
 
-    def project(xq, i):
-        two = pl.ds(xq * 2, 2)
+    def project(at, i):
+        two = pl.ds(at, 2)
 
         @loop(n_t)
         def _(t):
@@ -380,40 +374,43 @@
 
         remote(up.at[two, o], ur.at[two], up_s.at[i], up_r.at[i], sib)
 
-    def project_sum(xq, i):
-        two = pl.ds(xq * 2, 2)
+    def project_sum(at, i):
+        two = pl.ds(at, 2)
         landed(ur.at[two], up_r.at[i])
         us[two] = (up[two, c] + ur[two]).astype(bf16)
 
+    def project_own():
+        project(OWN, 0)
+
     def project_near():
-        project(xi, 0)
-        project(xl, 1)
-        project(xr, 2)
+        project(RIGHT, 1)
+        project(LEFT, 2)
+
+    def project_far():
+        landed(agx.at[FAR + 1, 0], agx_r.at[6])
+        landed(agx.at[FAR + 1, 1], agx_r.at[8])
+        project(FAR, 3)
+
+    def update_out(ks):
+        for k in ks:
+            remote(us.at[k], uin.at[d], up_s.at[3 + k], up_r.at[3 + there[k]], (p, peers[k], c))
 
     def update_near():
-        project_sum(xi, 0)
-        project_sum(xl, 1)
-        project_sum(xr, 2)
-        uin[d] = us[d]
-        remote(us.at[dz], uin.at[d], up_s.at[4], up_r.at[4], zdev)
-        remote(us.at[dl], uin.at[d], up_s.at[5], up_r.at[5], left)
-        remote(us.at[dr], uin.at[d], up_s.at[6], up_r.at[6], right)
-        remote(us.at[dlz], uin.at[d], up_s.at[7], up_r.at[7], (p, dlz, c))
-        remote(us.at[drz], uin.at[d], up_s.at[8], up_r.at[8], (p, drz, c))
+        project_sum(OWN, 0)
+        project_sum(RIGHT, 1)
+        project_sum(LEFT, 2)
+        uin[d] = us[OWN]
+        update_out((1, 2, 4, 3, 5))
 
     def update_far():
-        landed(agx.at[dx2z, 0], agx_r.at[6])
-        landed(agx.at[dx2z, 1], agx_r.at[8])
-        project(x2, 3)
-        project_sum(x2, 3)
-        remote(us.at[dx2], uin.at[d], up_s.at[9], up_r.at[9], (p, dx2, c))
-        remote(us.at[dx2z], uin.at[d], up_s.at[10], up_r.at[10], (p, dx2z, c))
+        project_sum(FAR, 3)
+        update_out((6, 7))
 
     mine = pl.ds(pl.multiple_of(c * 64, 64), 64)
 
     def output():
-        for k, at in ((4, dz), (5, dr), (6, dl), (7, drz), (8, dlz), (9, dx2), (10, dx2z)):
-            landed(uin.at[at], up_r.at[k])
+        for k in range(1, 8):
+            landed(uin.at[peers[k]], up_r.at[3 + k])
 
         @loop(8)
         def _(q):
@@ -449,13 +446,13 @@
         ends.append(local(gsum, gg_hbm.at[:, half_c], out_sem.at[2]))
         remote(gsum, gg_hbm.at[:, half_c], sib_s.at[6], sib_r.at[6], sib)
 
-    def weight_part(xq, first):
-        two = pl.ds(xq * 2, 2)
+    def weight_part(at, n, first):
+        some = pl.ds(at, n)
 
         @loop(n_t)
         def _(t):
             val = lax.dot_general(
-                ago[two, :, :, cols(t)].reshape(256, CT), gc[two].reshape(256, oc),
+                ago[some, :, :, cols(t)].reshape(128 * n, CT), gc[some].reshape(128 * n, oc),
                 (((0,), (0,)), ((), ())), preferred_element_type=f32,
             )
             if first:
@@ -464,26 +461,25 @@
                 wg[cols(t), :] = wg[cols(t), :] + val
 
     def weight_own():
-        weight_part(xi, True)
+        weight_part(OWN, 2, True)
 
     def weight_near():
-        weight_part(xl, False)
-        weight_part(xr, False)
+        weight_part(RIGHT, 4, False)
         ends.append(local(wg, wg_hbm, out_sem.at[3]))
-        ends.append(local(gc.at[pl.ds(x2 * 2, 2)], gc2_hbm, out_sem.at[4]))
+        ends.append(local(gc.at[pl.ds(FAR, 2)], gc2_hbm, out_sem.at[4]))
 
     def weight_rows():
         for n in (6, 8, 9, 11):
-            landed(ago.at[dx2z, 0, pl.ds(0, 32)], ago_r.at[n])
-        ends.append(local(ago.at[pl.ds(x2 * 2, 2)], ago2_hbm, out_sem.at[5]))
+            landed(ago.at[FAR + 1, 0, pl.ds(0, 32)], ago_r.at[n])
+        ends.append(local(ago.at[pl.ds(FAR, 2)], ago2_hbm, out_sem.at[5]))
 
     ends = []
     for step in (
-        grads_out, norm_new, stash_out, new_x, grads_sib, new_z, grads_in, sum_far_z,
-        sum_near_z, new_far, sum_near, new_zx, new_far_z, park_out, sum_far, norm_old,
-        sum_through, new_near, old_x, old_z, project_near, park_sib, update_far, old_far,
-        old_zx, weight_own, sum_z, update_near, sum_own, old_far_z, input_out, output,
-        old_far_x, weight_near, gain_out, weight_rows,
+        grads_out, norm_new, stash_out, new_z, new_x, new_far, grads_sib, grads_in,
+        sum_first, sum_near, sum_near_z, new_zx, norm_old, new_far_z, sum_far, park_out,
+        old_z, old_x, sum_through, old_zx, weight_own, old_far, sum_z, project_own,
+        new_near, project_near, update_near, sum_own, old_far_z, project_far, input_out,
+        update_far, old_far_x, park_sib, weight_near, gain_out, output, weight_rows,
     ):
         step()
 
@@ -580,6 +576,7 @@
             vm((2, 2, 64, hc), bf16),
             vm((rows, hc), bf16),
             vm((rows, hc), bf16),
+            vm((4, 2, 64, hc), f32),
             vm((rows, hc), f32),
             vm((2, rows, 128), f32),
             vm((2, rows, 128), f32),

time: 162 us -> 155 us (0.957); the launches traced: 161 us -> 152 us
  Pallas kernels: 160 us -> 151 us
    pallas_call x1, Pallas kernels: 151 us -> 142 us  [local(): pl.pallas_call(kernel, out_shape=(jax.ShapeDtypeStruct((rows, width), bf1...]
where the time goes in v3:
time: 155 us; the launch traced here: 152 us
  Pallas kernels  151 us (97%)
    pallas_call x1, Pallas kernels, local(): pl.pallas_call(kernel, out_shape=(jax.ShapeDtypeStruct((rows, width), bf1...  142 us
    pallas_call x1, Pallas kernels, local(): pl.pallas_call(finish, out_shape=(jax.ShapeDtypeStruct((rows, width), bf1...  9.45 us

profile of v3, /device:TPU:9, one launch (start us, length us, event | category | flops | bytes accessed | tf_op | source)
XLA Modules:
  0.0 151.9 jit_solution(17298362448193256600)
XLA Ops:
  0.6 141.9 %relay_step.1 = (bf16[128,5120]{1,0:T(8,128)(2,1)}, bf16[128,5120]{1,0:T(8,128)(2,1)}, f32[2560,640]{1,0:T(8,128)}, f32[1,5120]{1,0:T(1,128)}, bf16[8,2,16,5120]...) custom-call(bf16[128,5120]{1,0:T(8,128)(2,1)} %bitcast.19, ...), custom_call_target="tpu_custom_call" | custom-call | flops 10737418240 | bytes 41943040 | tf_op jit(solution)/shard_map/relay_step/pallas_call | solution.py:540
  142.5 9.4 %finish.1 = (bf16[128,5120]{1,0:T(8,128)(2,1)}, bf16[128,5120]{1,0:T(8,128)(2,1)}, f32[1,5120]{1,0:T(1,128)}, bf16[8,2,16,5120]{3,2,1,0:T(8,128)(2,1)}, f32[2560,640]{1,0:T(8,128)}) custom-call(bf16[128,5120]{1,0:T(8,128)(2,1)} %get-tuple-element.17.so_in, bf16[128,5120]{1,0:T(8,128)(2,1)} %get-tuple-element.18.ig_in, f32[1,5120]{1,0:T(1,128)} %get-tuple-element.19.gg_in, ...), custom_call_target="tpu_custom_call" | custom-call | flops 1073741824 | bytes 26214400 | tf_op jit(solution)/shard_map/finish/pallas_call | solution.py:613

commit v4 on v3

--- a/solution.py
+++ b/solution.py
@@ -16,10 +16,10 @@
 
 def kernel(
     x_hbm, blocks_hbm, grad_hbm, gain_hbm, w_hbm, parked_hbm, flight, hosts_old, hosts_new,
-    so_hbm, ig_hbm, wg_hbm, gg_hbm, pn_hbm, ago2_hbm, gc2_hbm,
-    xf, xh, gh, gain, w, stage, p1s, p1r, early, oscale, p2s, p2r, gc,
+    so_out, ig_out, wg_out, gg_out, pn_out, ago2_out, gc2_out,
+    xf, xh, gh, gain, w, stage, p1s, p1r, early, oscale, p2s, gc,
     agx, ago, a2, b_r, b_l, rz2, rl2, rr2, rl1, rr1, zs, zr, sums, ng,
-    part, sib_part, up, ur, us, uin, so, ig, wg, gp, gsum,
+    part, sib_part, up, ur, us, uin, gp,
     local_sem, a2a_s, a2a_r, p1_s, p1_r, p2_s, p2_r, agx_s, agx_r, ago_s, ago_r,
     rs_s, rs_r, sib_s, sib_r, up_s, up_r, gg_s, gg_r, out_sem,
 ):
@@ -65,6 +65,12 @@
         cp.start()
         return cp
 
+    barrier = pltpu.get_barrier_semaphore()
+    for k in range(1, 8):
+        pl.semaphore_signal(barrier, inc=1, device_id=(pipe_peer(k), d, c), device_id_type=MESH)
+        pl.semaphore_signal(barrier, inc=1, device_id=(p, dp_peer(k), c), device_id_type=MESH)
+    pl.semaphore_signal(barrier, inc=1, device_id=sib, device_id_type=MESH)
+
     c_gown = local(
         grad_hbm.at[pl.ds(c * 64, 64), pl.ds(pl.multiple_of(d * oc, 128), oc)],
         gc.at[OWN, c], local_sem.at[6],
@@ -72,16 +78,8 @@
     c_xf = local(x_hbm, xf, local_sem.at[0])
     c_xh = local(blocks_hbm.at[:, :, half_c], xh.at[pl.ds(0, 8)], local_sem.at[1])
     c_gain = local(gain_hbm.at[:, half_c], gain, local_sem.at[2])
-    c_stage = local(parked_hbm.at[:, :, :, :, half_c], stage, local_sem.at[3])
-    c_w = local(w_hbm, w, local_sem.at[4])
-    c_gh = local(grad_hbm.at[:, half_c], gh, local_sem.at[5])
-    later = []
-
-    barrier = pltpu.get_barrier_semaphore()
-    for k in range(1, 8):
-        pl.semaphore_signal(barrier, inc=1, device_id=(pipe_peer(k), d, c), device_id_type=MESH)
-        pl.semaphore_signal(barrier, inc=1, device_id=(p, dp_peer(k), c), device_id_type=MESH)
-    pl.semaphore_signal(barrier, inc=1, device_id=sib, device_id_type=MESH)
+    later, loads = [], {}
+
     pl.semaphore_wait(barrier, 15)
 
     def cols(t):
@@ -127,6 +125,7 @@
                 grad_hbm.at[pl.ds(c * 64, 64), pl.ds(pl.multiple_of(q * oc, 128), oc)],
                 gc.at[there[k], c], a2a_s.at[k], a2a_r.at[there[k]], (p, q, c),
             )
+        loads["stage"] = local(parked_hbm.at[:, :, :, :, half_c], stage, local_sem.at[3])
 
     def grads_sib():
         c_gown.wait()
@@ -135,13 +134,15 @@
         remote(gc.at[:, c], gc.at[:, c], sib_s.at[0], sib_r.at[0], sib)
 
     def grads_in():
-        c_w.wait()
+        loads["w"].wait()
+        loads["gh"] = local(grad_hbm.at[:, half_c], gh, local_sem.at[5])
         landed(gc.at[:, o], sib_r.at[0])
 
     def norm_new():
         c_xf.wait()
         c_xh.wait()
         c_gain.wait()
+        loads["w"] = local(w_hbm, w, local_sem.at[4])
 
         @loop(8)
         def _(i):
@@ -194,7 +195,7 @@
         near_z(agx, agx_r)
 
     def stash_out():
-        c_stage.wait()
+        loads["stage"].wait()
 
         @loop(8)
         def _(s):
@@ -243,15 +244,16 @@
         for h, n in ((0, 5), (1, 7)):
             landed(ago.at[FAR, h], ago_r.at[n])
             remote(
-                ago.at[FAR, h, pl.ds(32, 32)], ago.at[FAR + 1, h, pl.ds(32, 32)],
+                ago.at[FAR, h, pl.ds(32, 32)], ago2_out.at[1, h, pl.ds(32, 32)],
                 ago_s.at[n + 4], ago_r.at[n + 4], zdev,
             )
+        ends.append(local(ago.at[FAR], ago2_out.at[0], out_sem.at[1]))
 
     def old_far_x():
         near_z(ago, ago_r)
         for h, n, at, to in ((0, 6, LEFT + 1, right), (1, 8, RIGHT + 1, left)):
             remote(
-                ago.at[at, h, pl.ds(0, 32)], ago.at[FAR + 1, h, pl.ds(0, 32)],
+                ago.at[at, h, pl.ds(0, 32)], ago2_out.at[1, h, pl.ds(0, 32)],
                 ago_s.at[n], ago_r.at[n], to,
             )
 
@@ -263,15 +265,14 @@
             p2s[slot // 2, slot % 2] = xh[which]
         for k in range(1, 8):
             q = pipe_peer(k)
-            remote(p2s.at[q], p2r.at[p], p2_s.at[k], p2_r.at[k], (q, d, c))
-        later.append(local(p2s.at[p], p2r.at[p], local_sem.at[8]))
+            remote(p2s.at[q], pn_out.at[p, :, :, half_c], p2_s.at[k], p2_r.at[k], (q, d, c))
+        later.append(local(p2s.at[p], pn_out.at[p, :, :, half_c], local_sem.at[8]))
 
     def park_sib():
         later.pop(0).wait()
         for k in range(1, 8):
-            landed(p2r.at[lax.rem(p + 8 - k, 8)], p2_r.at[k])
-        ends.append(local(p2r, pn_hbm.at[:, :, :, half_c], out_sem.at[6]))
-        remote(p2r, pn_hbm.at[:, :, :, half_c], sib_s.at[2], sib_r.at[2], sib)
+            landed(pn_out.at[lax.rem(p + 8 - k, 8), :, :, half_c], p2_r.at[k])
+        remote(pn_out.at[:, :, :, half_c], pn_out.at[:, :, :, half_c], sib_s.at[2], sib_r.at[2], sib)
 
     def sum_first():
         @loop(n_t)
@@ -415,14 +416,13 @@
         @loop(8)
         def _(q):
             at = pl.ds(pl.multiple_of(q * oc, 128), oc)
-            so[:, at] = (xf[mine, at].astype(f32) + uin[q].astype(f32)).astype(bf16)
-
-        ends.append(local(so, so_hbm.at[mine, :], out_sem.at[0]))
-        remote(so, so_hbm.at[mine, :], sib_s.at[4], sib_r.at[4], sib)
+            so_out[mine, at] = (xf[mine, at].astype(f32) + uin[q].astype(f32)).astype(bf16)
+
+        remote(so_out.at[mine, :], so_out.at[mine, :], sib_s.at[4], sib_r.at[4], sib)
 
     def input_out():
         landed(sib_part.at[1], sib_r.at[3])
-        c_gh.wait()
+        loads["gh"].wait()
 
         @loop(8)
         def _(i):
@@ -431,10 +431,9 @@
             scale = oscale[rows, 0:1]
             old_hat = early[rows, :].astype(f32) * scale
             centred = ng[rows, :] * gain[...] - old_hat * mean
-            ig[rows, :] = (gh[rows, :].astype(f32) + scale * centred).astype(bf16)
-
-        ends.append(local(ig, ig_hbm.at[:, half_c], out_sem.at[1]))
-        remote(ig, ig_hbm.at[:, half_c], sib_s.at[5], sib_r.at[5], sib)
+            ig_out[rows, half_c] = (gh[rows, :].astype(f32) + scale * centred).astype(bf16)
+
+        remote(ig_out.at[:, half_c], ig_out.at[:, half_c], sib_s.at[5], sib_r.at[5], sib)
 
     def gain_out():
         for k in range(1, 8):
@@ -442,9 +441,8 @@
         total = gp[0]
         for q in range(1, 8):
             total = total + gp[q]
-        gsum[...] = total
-        ends.append(local(gsum, gg_hbm.at[:, half_c], out_sem.at[2]))
-        remote(gsum, gg_hbm.at[:, half_c], sib_s.at[6], sib_r.at[6], sib)
+        gg_out[:, half_c] = total
+        remote(gg_out.at[:, half_c], gg_out.at[:, half_c], sib_s.at[6], sib_r.at[6], sib)
 
     def weight_part(at, n, first):
         some = pl.ds(at, n)
@@ -456,38 +454,36 @@
                 (((0,), (0,)), ((), ())), preferred_element_type=f32,
             )
             if first:
-                wg[cols(t), :] = val
+                wg_out[cols(t), :] = val
             else:
-                wg[cols(t), :] = wg[cols(t), :] + val
+                wg_out[cols(t), :] = wg_out[cols(t), :] + val
 
     def weight_own():
         weight_part(OWN, 2, True)
 
     def weight_near():
         weight_part(RIGHT, 4, False)
-        ends.append(local(wg, wg_hbm, out_sem.at[3]))
-        ends.append(local(gc.at[pl.ds(FAR, 2)], gc2_hbm, out_sem.at[4]))
+        ends.append(local(gc.at[pl.ds(FAR, 2)], gc2_out, out_sem.at[0]))
 
     def weight_rows():
         for n in (6, 8, 9, 11):
-            landed(ago.at[FAR + 1, 0, pl.ds(0, 32)], ago_r.at[n])
-        ends.append(local(ago.at[pl.ds(FAR, 2)], ago2_hbm, out_sem.at[5]))
+            landed(ago2_out.at[1, 0, pl.ds(0, 32)], ago_r.at[n])
 
     ends = []
     for step in (
-        grads_out, norm_new, stash_out, new_z, new_x, new_far, grads_sib, grads_in,
-        sum_first, sum_near, sum_near_z, new_zx, norm_old, new_far_z, sum_far, park_out,
-        old_z, old_x, sum_through, old_zx, weight_own, old_far, sum_z, project_own,
-        new_near, project_near, update_near, sum_own, old_far_z, project_far, input_out,
-        update_far, old_far_x, park_sib, weight_near, gain_out, output, weight_rows,
+        grads_out, norm_new, stash_out, new_x, grads_sib, grads_in, new_far, new_z,
+        sum_first, sum_near_z, norm_old, old_x, new_zx, old_z, sum_far, park_out,
+        sum_through, old_zx, new_far_z, sum_near, old_far, sum_z, new_near, project_own,
+        project_near, update_near, project_far, old_far_z, park_sib, weight_own, sum_own,
+        update_far, old_far_x, weight_near, input_out, output, weight_rows, gain_out,
     ):
         step()
 
     half_o = pl.ds(pl.multiple_of(o * hc, 128), hc)
-    landed(pn_hbm.at[:, :, :, half_o], sib_r.at[2])
-    landed(so_hbm.at[pl.ds(pl.multiple_of(o * 64, 64), 64), :], sib_r.at[4])
-    landed(ig_hbm.at[:, half_o], sib_r.at[5])
-    landed(gg_hbm.at[:, half_o], sib_r.at[6])
+    landed(pn_out.at[:, :, :, half_o], sib_r.at[2])
+    landed(so_out.at[pl.ds(pl.multiple_of(o * 64, 64), 64), :], sib_r.at[4])
+    landed(ig_out.at[:, half_o], sib_r.at[5])
+    landed(gg_out.at[:, half_o], sib_r.at[6])
     for cp in ends:
         cp.wait()
     for cp in sends:
@@ -495,36 +491,24 @@
 
 
 def finish(
-    so_in, ig_in, gg_in, pn_in, part, rows, grads, so, ig, gg, pn, wg,
-    v_so, v_ig, v_gg, v_pn, v_wg, v_rows, v_grads, in_sem, out_sem,
+    so_in, ig_in, gg_in, pn_in, part, rows, grads, so, ig, gg, pn, wg, v_wg, out_sem,
 ):
-    tiles = [pl.ds(t * CT, CT) for t in range(part.shape[0] // CT)]
-    halves = [pl.ds(i * 4, 4) for i in range(2)]
-    moves = [(part.at[t], v_wg.at[t], wg.at[t]) for t in tiles]
-    plain = [(so_in, v_so, so), (ig_in, v_ig, ig), (gg_in, v_gg, gg)]
-    plain += [(pn_in.at[h], v_pn.at[h], pn.at[h]) for h in halves]
-    order = []
-    for i in range(len(tiles)):
-        order += [(i, moves[i]), (len(tiles) + i, plain[i])]
-
     def copy(src, dst, sem):
         cp = pltpu.make_async_copy(src, dst, sem)
         cp.start()
         return cp
 
-    first = [copy(rows, v_rows, in_sem.at[10]), copy(grads, v_grads, in_sem.at[11])]
-    loads = [copy(src, mid, in_sem.at[i]) for i, (src, mid, _) in order]
-    for cp in first:
-        cp.wait()
-    stores = []
-    for (i, (_, mid, dst)), load in zip(order, loads):
-        load.wait()
-        if i < len(tiles):
-            mid[...] = mid[...] + lax.dot_general(
-                v_rows[:, tiles[i]], v_grads[...], (((0,), (0,)), ((), ())),
-                preferred_element_type=jnp.float32,
-            )
-        stores.append(copy(mid, dst, out_sem.at[i]))
+    plain = [(so_in, so), (ig_in, ig), (gg_in, gg), (pn_in, pn)]
+    stores = [copy(src, dst, out_sem.at[i]) for i, (src, dst) in enumerate(plain)]
+    left = rows[...].reshape(256, part.shape[0])
+    right = grads[...].reshape(256, part.shape[1])
+    for t in range(part.shape[0] // CT):
+        at = pl.ds(t * CT, CT)
+        v_wg[at, :] = part[at, :] + lax.dot_general(
+            left[:, t * CT:(t + 1) * CT], right, (((0,), (0,)), ((), ())),
+            preferred_element_type=jnp.float32,
+        )
+        stores.append(copy(v_wg.at[at], wg.at[at], out_sem.at[len(plain) + t]))
     for cp in stores:
         cp.wait()
 
@@ -536,20 +520,21 @@
     hbm = pl.BlockSpec(memory_space=pl.ANY)
     smem = pl.BlockSpec(memory_space=pltpu.SMEM)
     vm = pltpu.VMEM
+    vmem = pl.BlockSpec(memory_space=pltpu.VMEM)
     dma = pltpu.SemaphoreType.DMA
     so_p, ig_p, wg_p, gg_p, pn_p, rows_p, grads_p = pl.pallas_call(
         kernel,
         out_shape=(
-            jax.ShapeDtypeStruct((rows, width), bf16),
-            jax.ShapeDtypeStruct((rows, width), bf16),
-            jax.ShapeDtypeStruct((hc, oc), f32),
-            jax.ShapeDtypeStruct((1, width), f32),
-            jax.ShapeDtypeStruct((8, 2, 16, width), bf16),
-            jax.ShapeDtypeStruct((2, 2, 64, hc), bf16),
-            jax.ShapeDtypeStruct((2, 2, 64, oc), bf16),
+            vm((rows, width), bf16),
+            vm((rows, width), bf16),
+            vm((hc, oc), f32),
+            vm((1, width), f32),
+            vm((8, 2, 16, width), bf16),
+            vm((2, 2, 64, hc), bf16),
+            vm((2, 2, 64, oc), bf16),
         ),
         in_specs=[hbm] * 6 + [smem] * 3,
-        out_specs=(hbm,) * 7,
+        out_specs=(vmem,) * 7,
         scratch_shapes=[
             vm((rows, width), bf16),
             vm((9, 16, hc), bf16),
@@ -561,7 +546,6 @@
             vm((16, 16, hc), bf16),
             vm((rows, hc), bf16),
             vm((rows, 128), f32),
-            vm((8, 2, 16, hc), bf16),
             vm((8, 2, 16, hc), bf16),
             vm((8, 2, 64, oc), bf16),
             vm((8, 2, 64, hc), bf16),
@@ -584,11 +568,7 @@
             vm((8, 64, oc), f32),
             vm((8, 64, oc), bf16),
             vm((8, 64, oc), bf16),
-            vm((64, width), bf16),
-            vm((rows, hc), bf16),
-            vm((hc, oc), f32),
             vm((8, 1, hc), f32),
-            vm((1, hc), f32),
             dma((9,)),
             dma((8,)), dma((8,)),
             dma((8,)), dma((8,)),
@@ -599,10 +579,10 @@
             dma((7,)), dma((7,)),
             dma((11,)), dma((11,)),
             dma((8,)), dma((8,)),
-            dma((7,)),
+            dma((2,)),
         ],
         compiler_params=pltpu.CompilerParams(
-            collective_id=0, has_side_effects=True, vmem_limit_bytes=62 * 2**20
+            collective_id=0, has_side_effects=True, vmem_limit_bytes=51 * 2**20
         ),
         cost_estimate=pl.CostEstimate(flops=10 * 2**30, bytes_accessed=40 * 2**20, transcendentals=0),
         name="relay_step",
@@ -619,23 +599,13 @@
             jax.ShapeDtypeStruct((8, 2, 16, width), bf16),
             jax.ShapeDtypeStruct((hc, oc), f32),
         ),
-        in_specs=[hbm] * 7,
+        in_specs=[vmem] * 7,
         out_specs=[hbm] * 5,
-        scratch_shapes=[
-            vm((rows, width), bf16),
-            vm((rows, width), bf16),
-            vm((1, width), f32),
-            vm((8, 2, 16, width), bf16),
-            vm((hc, oc), f32),
-            vm((256, hc), bf16),
-            vm((256, oc), bf16),
-            dma((12,)),
-            dma((10,)),
-        ],
-        compiler_params=pltpu.CompilerParams(vmem_limit_bytes=62 * 2**20),
-        cost_estimate=pl.CostEstimate(flops=2**30, bytes_accessed=25 * 2**20, transcendentals=0),
+        scratch_shapes=[vm((hc, oc), f32), dma((9,))],
+        compiler_params=pltpu.CompilerParams(vmem_limit_bytes=32 * 2**20),
+        cost_estimate=pl.CostEstimate(flops=2**30, bytes_accessed=12 * 2**20, transcendentals=0),
         name="finish",
-    )(so_p, ig_p, gg_p, pn_p, wg_p, rows_p.reshape(256, hc), grads_p.reshape(256, oc))
+    )(so_p, ig_p, gg_p, pn_p, wg_p, rows_p, grads_p)
     return so[None], ig[None], wg[None], gg, pn[None]
 
 

time: 155 us -> 149 us (0.961)
  Pallas kernels: 151 us -> 147 us
    pallas_call x1, Pallas kernels: 9.45 us -> 4.46 us  [local(): pl.pallas_call(finish, out_shape=(jax.ShapeDtypeStruct((rows, width), bf1...]
where the time goes in v4:
time: 149 us; the launch traced here: 147 us
  Pallas kernels  147 us (99%)
    pallas_call x1, Pallas kernels, local(): pl.pallas_call(kernel, out_shape=(vm((rows, width), bf16), vm((rows, widt...  142 us
    pallas_call x1, Pallas kernels, local(): pl.pallas_call(finish, out_shape=(jax.ShapeDtypeStruct((rows, width), bf1...  4.46 us

profile of v4, /device:TPU:9, one launch (start us, length us, event | category | flops | bytes accessed | tf_op | source)
XLA Modules:
  0.0 147.4 jit_solution(8434491575830652923)
XLA Ops:
  0.6 142.3 %relay_step.1 = (bf16[128,5120]{1,0:T(8,128)(2,1)S(1)}, bf16[128,5120]{1,0:T(8,128)(2,1)S(1)}, f32[2560,640]{1,0:T(8,128)S(1)}, f32[1,5120]{1,0:T(1,128)S(1)}, b...) custom-call(bf16[128,5120]{1,0:T(8,128)(2,1)} %bitcast.15, ...), custom_call_target="tpu_custom_call" | custom-call | flops 10737418240 | bytes 41943040 | tf_op jit(solution)/shard_map/relay_step/pallas_call | solution.py:525
  142.9 4.5 %finish.1 = (bf16[128,5120]{1,0:T(8,128)(2,1)}, bf16[128,5120]{1,0:T(8,128)(2,1)}, f32[1,5120]{1,0:T(1,128)}, bf16[8,2,16,5120]{3,2,1,0:T(8,128)(2,1)}, f32[2560,640]{1,0:T(8,128)}) custom-call(bf16[128,5120]{1,0:T(8,128)(2,1)S(1)} %get-tuple-element.17.so_in, bf16[128,5120]{1,0:T(8,128)(2,1)S(1)} %get-tuple-element.18.ig_in, ...), custom_call_target="tpu_custom_call" | custom-call | flops 1073741824 | bytes 12582912 | tf_op jit(solution)/shard_map/finish/pallas_call | solution.py:593

commit v5 on v4

--- a/solution.py
+++ b/solution.py
@@ -244,7 +244,7 @@
         for h, n in ((0, 5), (1, 7)):
             landed(ago.at[FAR, h], ago_r.at[n])
             remote(
-                ago.at[FAR, h, pl.ds(32, 32)], ago2_out.at[1, h, pl.ds(32, 32)],
+                ago.at[FAR, h, pl.ds(48, 16)], ago2_out.at[1, h, pl.ds(48, 16)],
                 ago_s.at[n + 4], ago_r.at[n + 4], zdev,
             )
         ends.append(local(ago.at[FAR], ago2_out.at[0], out_sem.at[1]))
@@ -253,7 +253,7 @@
         near_z(ago, ago_r)
         for h, n, at, to in ((0, 6, LEFT + 1, right), (1, 8, RIGHT + 1, left)):
             remote(
-                ago.at[at, h, pl.ds(0, 32)], ago2_out.at[1, h, pl.ds(0, 32)],
+                ago.at[at, h, pl.ds(0, 48)], ago2_out.at[1, h, pl.ds(0, 48)],
                 ago_s.at[n], ago_r.at[n], to,
             )
 
@@ -355,56 +355,55 @@
         for k in range(1, 8):
             remote(gp.at[d], gp.at[d], gg_s.at[k], gg_r.at[k], (p, dp_peer(k), c))
 
-    def project(at, i):
-        two = pl.ds(at, 2)
-
-        @loop(n_t)
+    def project(at, n, i):
+        some = pl.ds(at, n)
+
+        @loop(2)
         def _(t):
+            half = pl.ds(pl.multiple_of(t * (hc // 2), 128), hc // 2)
             val = jnp.dot(
-                agx[two, :, :, cols(t)].reshape(256, CT), w[cols(t), :],
+                agx[some, :, :, half].reshape(128 * n, hc // 2), w[half, :],
                 preferred_element_type=f32,
-            ).reshape(2, 2, 64, oc)
+            ).reshape(n, 2, 64, oc)
 
             @pl.when(t == 0)
             def _():
-                up[two] = val
+                up[some] = val
 
             @pl.when(t > 0)
             def _():
-                up[two] = up[two] + val
-
-        remote(up.at[two, o], ur.at[two], up_s.at[i], up_r.at[i], sib)
-
-    def project_sum(at, i):
-        two = pl.ds(at, 2)
-        landed(ur.at[two], up_r.at[i])
-        us[two] = (up[two, c] + ur[two]).astype(bf16)
+                up[some] = up[some] + val
+
+        remote(up.at[some, o], ur.at[some], up_s.at[i], up_r.at[i], sib)
+
+    def project_sum(at, n, i):
+        some = pl.ds(at, n)
+        landed(ur.at[some], up_r.at[i])
+        us[some] = (up[some, c] + ur[some]).astype(bf16)
 
     def project_own():
-        project(OWN, 0)
+        project(OWN, 2, 0)
 
     def project_near():
-        project(RIGHT, 1)
-        project(LEFT, 2)
+        project(RIGHT, 4, 1)
 
     def project_far():
         landed(agx.at[FAR + 1, 0], agx_r.at[6])
         landed(agx.at[FAR + 1, 1], agx_r.at[8])
-        project(FAR, 3)
+        project(FAR, 2, 3)
 
     def update_out(ks):
         for k in ks:
             remote(us.at[k], uin.at[d], up_s.at[3 + k], up_r.at[3 + there[k]], (p, peers[k], c))
 
     def update_near():
-        project_sum(OWN, 0)
-        project_sum(RIGHT, 1)
-        project_sum(LEFT, 2)
+        project_sum(OWN, 2, 0)
+        project_sum(RIGHT, 4, 1)
         uin[d] = us[OWN]
         update_out((1, 2, 4, 3, 5))
 
     def update_far():
-        project_sum(FAR, 3)
+        project_sum(FAR, 2, 3)
         update_out((6, 7))
 
     mine = pl.ds(pl.multiple_of(c * 64, 64), 64)
@@ -466,16 +465,18 @@
         ends.append(local(gc.at[pl.ds(FAR, 2)], gc2_out, out_sem.at[0]))
 
     def weight_rows():
-        for n in (6, 8, 9, 11):
-            landed(ago2_out.at[1, 0, pl.ds(0, 32)], ago_r.at[n])
+        for n in (6, 8):
+            landed(ago2_out.at[1, 0, pl.ds(0, 48)], ago_r.at[n])
+        for n in (9, 11):
+            landed(ago2_out.at[1, 0, pl.ds(48, 16)], ago_r.at[n])
 
     ends = []
     for step in (
-        grads_out, norm_new, stash_out, new_x, grads_sib, grads_in, new_far, new_z,
-        sum_first, sum_near_z, norm_old, old_x, new_zx, old_z, sum_far, park_out,
-        sum_through, old_zx, new_far_z, sum_near, old_far, sum_z, new_near, project_own,
-        project_near, update_near, project_far, old_far_z, park_sib, weight_own, sum_own,
-        update_far, old_far_x, weight_near, input_out, output, weight_rows, gain_out,
+        grads_out, norm_new, stash_out, new_x, grads_sib, grads_in, sum_first, new_far,
+        sum_near_z, new_z, norm_old, old_x, sum_far, new_zx, old_z, park_out, sum_through,
+        old_zx, new_far_z, sum_near, old_far, sum_z, new_near, project_own, project_near,
+        update_near, project_far, old_far_z, park_sib, weight_own, sum_own, update_far,
+        old_far_x, weight_near, input_out, gain_out, output, weight_rows,
     ):
         step()
 

time: 149 us -> 149 us (level)
  no operation moved by 1% of the time
where the time goes in v5:
time: 149 us; the launch traced here: 148 us
  Pallas kernels  148 us (99%)
    pallas_call x1, Pallas kernels, local(): pl.pallas_call(kernel, out_shape=(vm((rows, width), bf16), vm((rows, widt...  143 us
    pallas_call x1, Pallas kernels, local(): pl.pallas_call(finish, out_shape=(jax.ShapeDtypeStruct((rows, width), bf1...  4.46 us

profile of v5, /device:TPU:9, one launch (start us, length us, event | category | flops | bytes accessed | tf_op | source)
XLA Modules:
  0.0 148.3 jit_solution(9114007156419429197)
XLA Ops:
  0.6 143.2 %relay_step.1 = (bf16[128,5120]{1,0:T(8,128)(2,1)S(1)}, bf16[128,5120]{1,0:T(8,128)(2,1)S(1)}, f32[2560,640]{1,0:T(8,128)S(1)}, f32[1,5120]{1,0:T(1,128)S(1)}, b...) custom-call(bf16[128,5120]{1,0:T(8,128)(2,1)} %bitcast.15, ...), custom_call_target="tpu_custom_call" | custom-call | flops 10737418240 | bytes 41943040 | tf_op jit(solution)/shard_map/relay_step/pallas_call | solution.py:526
  143.9 4.5 %finish.1 = (bf16[128,5120]{1,0:T(8,128)(2,1)}, bf16[128,5120]{1,0:T(8,128)(2,1)}, f32[1,5120]{1,0:T(1,128)}, bf16[8,2,16,5120]{3,2,1,0:T(8,128)(2,1)}, f32[2560,640]{1,0:T(8,128)}) custom-call(bf16[128,5120]{1,0:T(8,128)(2,1)S(1)} %get-tuple-element.17.so_in, bf16[128,5120]{1,0:T(8,128)(2,1)S(1)} %get-tuple-element.18.ig_in, ...), custom_call_target="tpu_custom_call" | custom-call | flops 1073741824 | bytes 12582912 | tf_op jit(solution)/shard_map/finish/pallas_call | solution.py:594
